TPU v7x, 32 devices: a whole 2x2x4 slice. The times are simulated.
32 devices in a mesh: rep: 2 (over x), walk: 16 (over z, y, core).
Axes of the slice: x: 2, y: 2, z: 4, core: 2. Of those that a mesh axis runs over, the one named last changes fastest.
Arguments:
- greens: bfloat16 [32, 64, 384], P(('rep', 'walk')), parts along dimension 0, may hold values from -6 to 6
- source: int32 [64], P(('rep', 'walk')), parts along dimension 0, may hold values from 0 to 15, as said below
- counts: int32 [32], P('rep'), parts along dimension 0, may hold values from 1 to 2, as said below
- cholesky: bfloat16 [512, 64, 384], P('walk'), may hold values from -0.0390625 to 0.0390625
Outputs:
- relocated: bfloat16 [64, 64, 384], P(('rep', 'walk')), parts along dimension 0
- exchange_energy: float32 [64], P(('rep', 'walk')), parts along dimension 0
- force_bias: float32 [64, 512], P(('rep', 'walk')), parts along dimension 0
There are 2 independent parts, one for each index of `rep`. A program takes and returns all parts, laid end to end along the dimension named above; an argument that names none is the same for every part. Nothing has to cross between parts.
Inputs may be any that keep to these rules, and one draw needn't show every extreme that they name: `source`: slot s belongs to walk device s div 2. Its walker comes from that device or one of the two devices beside it along the closed loop of walk devices. Slots beyond a device's count also name some walker. Slots 0 to counts[d] - 1 of device d are live.
All inputs are finite; a program needn't handle non-finite values.
Results may differ from a plain program's by a relative error of at most 0.001.
Values may be sent and summed in bfloat16 or wider, within the bound.
No kernel may reach another device: no remote copies, remote signals or barrier semaphores. Data moves between devices by JAX's collectives and lax.ppermute only.
A program may use at most 64 MiB of HBM per device.

v0:
```python
import jax
import jax.numpy as jnp
from jax import lax
from jax.sharding import PartitionSpec as P


def padded(block, sides, width):
    for axis, dim in sides:
        count = lax.axis_size(axis)
        forward = [(i, i + 1) for i in range(count - 1)]
        forward.append((count - 1, 0))
        backward = [(target, source) for source, target in forward]
        low = lax.ppermute(
            lax.slice_in_dim(block, block.shape[dim] - width, None, axis=dim), axis, forward
        )
        high = lax.ppermute(lax.slice_in_dim(block, 0, width, axis=dim), axis, backward)
        block = jnp.concatenate([low, block, high], axis=dim)
    return block


def body(greens, source, counts, cholesky):
    walkers = lax.axis_size("walk")
    my_index = lax.axis_index("walk")
    old_slots = greens.shape[0]
    new_slots = source.shape[0]
    chol_dev = cholesky.shape[0]
    occupied = cholesky.shape[1]
    orbitals = cholesky.shape[2]
    nchol = chol_dev * walkers
    nearby = padded(greens, (("walk", 0),), old_slots)
    src_dev = source // old_slots
    relative = (src_dev - my_index + 1) % walkers
    chosen = relative * old_slots + source % old_slots
    my_count = lax.dynamic_index_in_dim(counts, my_index, 0, keepdims=False)
    is_live = jnp.arange(new_slots) < my_count
    relocated = jnp.where(
        is_live[:, None, None], jnp.take(nearby, chosen, axis=0), jnp.zeros((), jnp.bfloat16)
    )
    chol_rows = cholesky.reshape(chol_dev, occupied * orbitals)
    batch_dims = (((2,), (2,)), ((0,), (0,)))

    def group_energy(group_in):
        members = group_in.shape[0]
        spread = jnp.broadcast_to(
            group_in[:, None], (members, chol_dev, occupied, orbitals)
        ).reshape(members * chol_dev, occupied, orbitals)
        stacked = jnp.broadcast_to(cholesky[None], (members, chol_dev, occupied, orbitals)).reshape(
            members * chol_dev, occupied, orbitals
        )
        forward = lax.dot_general(stacked, spread, batch_dims, preferred_element_type=jnp.float32)
        mirrored = lax.dot_general(spread, stacked, batch_dims, preferred_element_type=jnp.float32)
        return -(0.5 / nchol) * jnp.sum((forward * mirrored).reshape(members, -1), axis=1)

    block_in = lax.all_gather(greens, "walk", axis=0, tiled=True)
    total_rows = block_in.shape[0]
    group = 1
    for candidate in range(1, 5):
        if total_rows % candidate == 0:
            group = candidate
    grouped = block_in.reshape(total_rows // group, group, occupied, orbitals)
    energies = lax.map(group_energy, grouped).reshape(total_rows)
    biases = lax.dot_general(
        block_in.reshape(block_in.shape[0], occupied * orbitals),
        chol_rows,
        (((1,), (1,)), ((), ())),
        preferred_element_type=jnp.float32,
    )
    bias_mine, energy_cols = (
        lax.all_to_all(biases, "walk", split_axis=0, concat_axis=1, tiled=True),
        lax.all_to_all(energies[:, None], "walk", split_axis=0, concat_axis=1, tiled=True),
    )
    energy_mine = jnp.sum(energy_cols, axis=1)
    bias_near, energy_near = (
        padded(bias_mine, (("walk", 0),), old_slots),
        padded(energy_mine, (("walk", 0),), old_slots),
    )
    bias_rows = jnp.take(bias_near, chosen, axis=0)
    energy_slot = jnp.take(energy_near, chosen, axis=0)
    exchange_energy = jnp.where(is_live, energy_slot, 0.0)
    force_bias = jnp.where(is_live[:, None], bias_rows, 0.0)
    return (relocated, exchange_energy, force_bias)


def solution(mesh):
    return jax.shard_map(
        body,
        mesh=mesh,
        in_specs=(
            P(("rep", "walk"), None, None),
            P(("rep", "walk")),
            P("rep"),
            P("walk", None, None),
        ),
        out_specs=(P(("rep", "walk"), None, None), P(("rep", "walk")), P(("rep", "walk"), None)),
        check_vma=False,
    )
```

profile of v0, /device:TPU:0, one launch (start us, length us, event | category | flops | bytes accessed | tf_op | source)
XLA Modules:
  0.0 130.4 jit_solution(3880565610310121807)
XLA Ops:
  0.6 0.5 collective-permute-start
  1.1 5.1 %collective-permute-start.1 = (bf16[1,64,384]{2,1,0:T(8,128)(2,1)}, bf16[1,64,384]{2,1,0:T(8,128)(2,1)S(1)}, u32[]{:S(2)}, u32[]{:S(2)}) collective-permute-start(bf16[1,64,384]{2,1,0:T(8,128)(2,1)} %param.6), channel_id=1, source_target_pairs={{1,0},{2,1},{3,2},{4,3},{5,4},{6,5},{7,6},{8,7},{9,8},{10,9},{11,1... | collective-permute-start | bytes 147464 | tf_op jit(solution)/shard_map/ppermute | solution.py:16
  6.2 21.7 %all_gather.3 = bf16[16,64,384]{2,1,0:T(8,128)(2,1)S(1)} all-gather(bf16[1,64,384]{2,1,0:T(8,128)(2,1)} %param.6), channel_id=1, replica_groups=mesh['rep'=2,'walk'=16] {'walk'}, dimensions={0}, use_global_device_ids=true | all-gather | bytes 835584 | tf_op jit(solution)/shard_map/all_gather | solution.py:54
  27.9 68.6 %while.10 = (s32[]{:T(128)}, f32[4,4]{1,0:T(4,128)S(1)}, bf16[4,4,64,384]{3,2,1,0:T(8,128)(2,1)S(1)}, bf16[32,64,384]{2,1,0:T(8,128)(2,1)}, s32[]{:T(128)}, /*index=5*/f32[]{:T(128)}, s32[]{:T(128)}) while((s32[]{:T(128)}, f32[4,4]{1,0:T(4,128)S(1)}, bf16[4,4,64,384]{3,2,1,0:T(8,128)(2,1)S(1)}, bf16[32,64,384]{2,1,0:T(8,128)(2,1)}, s32[]{:T(128)}, ...), condition=%wide.region_3.4_spmd, body=%wide.region_0.3_spmd.sunk | while | flops 403701760 | bytes 44107972 | solution.py:61
  27.9 0.0 copy-start
  28.0 1.0 broadcast_in_dim.91
  29.0 0.4 copy-done
  29.4 1.0 broadcast_in_dim.92
  30.4 4.3 %fusion.14 = f32[128,64,64]{2,1,0:T(8,128)} fusion(bf16[128,64,384]{2,1,0:T(8,128)(2,1)S(1)} %bitcast.33, bf16[128,64,384]{2,1,0:T(8,128)(2,1)S(1)} %bitcast.34), kind=kOutput, calls=%fused_computation.24.clone.1 | convolution fusion | flops 402653184 | bytes 14680064 | tf_op jit(solution)/shard_map/while/body/eval_jaxpr/dot_general | solution.py:50
  34.7 5.7 %copy.25 = f32[128,64,64]{1,2,0:T(8,128)} copy(f32[128,64,64]{2,1,0:T(8,128)} %fusion.14) | data formatting | bytes 4194304 | tf_op jit(solution)/shard_map/while/body/eval_jaxpr/dot_general | solution.py:50
  40.3 4.5 %fusion.15 = f32[128]{0:T(128)S(1)} fusion(f32[128,64,64]{2,1,0:T(8,128)} %fusion.14, f32[128,64,64]{1,2,0:T(8,128)} %copy.25), kind=kLoop, calls=%fused_computation.4.clone.1 | loop fusion | flops 1048448 | bytes 4194816 | tf_op jit(solution)/shard_map/while/body/eval_jaxpr/reduce_sum | solution.py:52
  44.8 0.1 reduce_sum.34
  44.9 0.1 reduce_sum.35
  45.1 0.0 copy-start
  45.1 1.0 broadcast_in_dim.91
  46.2 0.3 copy-done
  46.5 1.0 broadcast_in_dim.92
  47.6 4.3 %fusion.14 = f32[128,64,64]{2,1,0:T(8,128)} fusion(bf16[128,64,384]{2,1,0:T(8,128)(2,1)S(1)} %bitcast.33, bf16[128,64,384]{2,1,0:T(8,128)(2,1)S(1)} %bitcast.34), kind=kOutput, calls=%fused_computation.24.clone.1 | convolution fusion | flops 402653184 | bytes 14680064 | tf_op jit(solution)/shard_map/while/body/eval_jaxpr/dot_general | solution.py:50
  51.8 5.7 %copy.25 = f32[128,64,64]{1,2,0:T(8,128)} copy(f32[128,64,64]{2,1,0:T(8,128)} %fusion.14) | data formatting | bytes 4194304 | tf_op jit(solution)/shard_map/while/body/eval_jaxpr/dot_general | solution.py:50
  57.5 4.5 %fusion.15 = f32[128]{0:T(128)S(1)} fusion(f32[128,64,64]{2,1,0:T(8,128)} %fusion.14, f32[128,64,64]{1,2,0:T(8,128)} %copy.25), kind=kLoop, calls=%fused_computation.4.clone.1 | loop fusion | flops 1048448 | bytes 4194816 | tf_op jit(solution)/shard_map/while/body/eval_jaxpr/reduce_sum | solution.py:52
  62.0 0.1 reduce_sum.34
  62.1 0.1 reduce_sum.35
  62.2 0.0 copy-start
  62.3 1.0 broadcast_in_dim.91
  63.3 0.3 copy-done
  63.7 1.0 broadcast_in_dim.92
  64.7 4.3 %fusion.14 = f32[128,64,64]{2,1,0:T(8,128)} fusion(bf16[128,64,384]{2,1,0:T(8,128)(2,1)S(1)} %bitcast.33, bf16[128,64,384]{2,1,0:T(8,128)(2,1)S(1)} %bitcast.34), kind=kOutput, calls=%fused_computation.24.clone.1 | convolution fusion | flops 402653184 | bytes 14680064 | tf_op jit(solution)/shard_map/while/body/eval_jaxpr/dot_general | solution.py:50
  69.0 5.7 %copy.25 = f32[128,64,64]{1,2,0:T(8,128)} copy(f32[128,64,64]{2,1,0:T(8,128)} %fusion.14) | data formatting | bytes 4194304 | tf_op jit(solution)/shard_map/while/body/eval_jaxpr/dot_general | solution.py:50
  74.6 4.5 %fusion.15 = f32[128]{0:T(128)S(1)} fusion(f32[128,64,64]{2,1,0:T(8,128)} %fusion.14, f32[128,64,64]{1,2,0:T(8,128)} %copy.25), kind=kLoop, calls=%fused_computation.4.clone.1 | loop fusion | flops 1048448 | bytes 4194816 | tf_op jit(solution)/shard_map/while/body/eval_jaxpr/reduce_sum | solution.py:52
  79.1 0.1 reduce_sum.34
  79.2 0.1 reduce_sum.35
  79.4 1.0 broadcast_in_dim.91
  80.5 0.3 copy-done
  80.8 1.0 broadcast_in_dim.92
  81.8 4.3 %fusion.14 = f32[128,64,64]{2,1,0:T(8,128)} fusion(bf16[128,64,384]{2,1,0:T(8,128)(2,1)S(1)} %bitcast.33, bf16[128,64,384]{2,1,0:T(8,128)(2,1)S(1)} %bitcast.34), kind=kOutput, calls=%fused_computation.24.clone.1 | convolution fusion | flops 402653184 | bytes 14680064 | tf_op jit(solution)/shard_map/while/body/eval_jaxpr/dot_general | solution.py:50
  86.1 5.7 %copy.25 = f32[128,64,64]{1,2,0:T(8,128)} copy(f32[128,64,64]{2,1,0:T(8,128)} %fusion.14) | data formatting | bytes 4194304 | tf_op jit(solution)/shard_map/while/body/eval_jaxpr/dot_general | solution.py:50
  91.8 4.5 %fusion.15 = f32[128]{0:T(128)S(1)} fusion(f32[128,64,64]{2,1,0:T(8,128)} %fusion.14, f32[128,64,64]{1,2,0:T(8,128)} %copy.25), kind=kLoop, calls=%fused_computation.4.clone.1 | loop fusion | flops 1048448 | bytes 4194816 | tf_op jit(solution)/shard_map/while/body/eval_jaxpr/reduce_sum | solution.py:52
  96.3 0.1 reduce_sum.34
  96.4 0.1 reduce_sum.35
  96.5 0.7 all_to_all.27
  97.2 3.5 %all-to-all-start = ((f32[16,1,1]{2,1,0:T(1,128)}), f32[16,1,1]{2,1,0:T(1,128)S(1)}, u32[]{:S(2)}, u32[]{:S(2)}) async-start(f32[16,1,1]{2,1,0:T(1,128)} %all_to_all.27), calls=%async_computation | async-start | bytes 16384 | tf_op jit(solution)/shard_map/all_to_all | solution.py:70
  100.7 3.7 %fusion.1 = f32[16,32,1]{1,0,2:T(8,128)} fusion(bf16[32,64,384]{2,1,0:T(8,128)(2,1)} %get-tuple-element.91, bf16[16,64,384]{2,1,0:T(8,128)(2,1)S(1)} %bitcast.36), kind=kOutput, calls=%fused_computation.7 | convolution fusion | flops 25165824 | bytes 2361344 | tf_op jit(solution)/shard_map/dot_general | solution.py:62
  104.4 0.6 dynamic_slice.8
  105.0 0.7 compare_and_fusion
  105.7 1.3 all-to-all-done
  107.0 4.7 %all-to-all-start.1 = ((f32[16,1,32]{2,1,0:T(1,128)}), f32[16,1,32]{2,1,0:T(1,128)S(1)}, u32[]{:S(2)}, u32[]{:S(2)}) async-start(f32[16,1,32]{2,1,0:T(1,128)} %bitcast.10), calls=%async_computation.1 | async-start | bytes 16384 | tf_op jit(solution)/shard_map/all_to_all | solution.py:69
  111.7 0.6 reduce_sum.25
  112.3 0.4 collective-permute-start.2
  112.7 4.0 %collective-permute-start.3 = (f32[1]{0:T(128)}, f32[1]{0:T(128)}, u32[]{:S(2)}, u32[]{:S(2)}) collective-permute-start(f32[1]{0:T(128)} %bitcast.7), channel_id=1, source_target_pairs={{1,0},{2,1},{3,2},{4,3},{5,4},{6,5},{7,6},{8,7},{9,8},{10,9},{11,1... | collective-permute-start | bytes 20 | tf_op jit(solution)/shard_map/ppermute | solution.py:16
  116.8 1.3 %collective-permute-done.2 = f32[1]{0:T(128)} collective-permute-done((f32[1]{0:T(128)}, f32[1]{0:T(128)}, u32[]{:S(2)}, u32[]{:S(2)}) %collective-permute-start.2) | collective-permute-done | bytes 36 | tf_op jit(solution)/shard_map/ppermute | solution.py:13
  118.1 0.1 collective-permute-done.3
  118.2 2.0 %pad_maximum_fusion.2 = f32[3]{0:T(128)S(1)} fusion(f32[1]{0:T(128)} %collective-permute-done.3, f32[1]{0:T(128)} %bitcast.7, f32[1]{0:T(128)} %collective-permute-done.2), kind=kLoop, calls=%fused_computation.21 | loop fusion | flops 6 | bytes 24 | tf_op jit(solution)/shard_map/concatenate | solution.py:17
  120.2 0.6 gather_fusion.1
  120.8 0.5 broadcast.101
  121.3 0.7 reduce.8
  122.0 0.1 all_to_all.26
  122.1 4.4 %collective-permute-start.5 = (f32[1,512]{1,0:T(1,128)S(1)}, f32[1,512]{1,0:T(1,128)S(1)}, u32[]{:S(2)}, u32[]{:S(2)}) collective-permute-start(f32[1,512]{1,0:T(1,128)S(1)} %all_to_all.26), channel_id=1, source_target_pairs={{1,0},{2,1},{3,2},{4,3},{5,4},{6,5},{7,6},{8,7},{9,8},{10,9},{11,1... | collective-permute-start | bytes 6152 | tf_op jit(solution)/shard_map/ppermute | solution.py:16
  126.5 1.2 select_select_fusion.2
  127.7 0.1 collective-permute-done.4
  127.8 0.0 collective-permute-done.5
  127.8 0.6 gather_fusion.2
  128.4 0.7 select_select_fusion.1
  129.1 0.6 gather_fusion
  129.7 0.7 select_select_fusion
  (27 shorter events, 0.3 us)
Async XLA Ops:
  0.6 128.4 %collective-permute-start = (bf16[1,64,384]{2,1,0:T(8,128)(2,1)}, bf16[1,64,384]{2,1,0:T(8,128)(2,1)S(1)}, u32[]{:S(2)}, u32[]{:S(2)}) collective-permute-start(bf16[1,64,384]{2,1,0:T(8,128)(2,1)} %param.6), channel_id=1, source_target_pairs={{0,1},{1,2},{2,3},{3,4},{4,5},{5,6},{6,7},{7,8},{8,9},{9,10},{10,1... | collective-permute-start | bytes 147464 | tf_op jit(solution)/shard_map/ppermute | solution.py:13
  1.1 127.9 %collective-permute-start.1 = (bf16[1,64,384]{2,1,0:T(8,128)(2,1)}, bf16[1,64,384]{2,1,0:T(8,128)(2,1)S(1)}, u32[]{:S(2)}, u32[]{:S(2)}) collective-permute-start(bf16[1,64,384]{2,1,0:T(8,128)(2,1)} %param.6), channel_id=1, source_target_pairs={{1,0},{2,1},{3,2},{4,3},{5,4},{6,5},{7,6},{8,7},{9,8},{10,9},{11,1... | collective-permute-start | bytes 147464 | tf_op jit(solution)/shard_map/ppermute | solution.py:16
  27.9 76.5 %copy-start.3 = (s32[16]{0:T(128)S(1)}, s32[16]{0:T(128)}, u32[]{:S(2)}) copy-start(s32[16]{0:T(128)} %param.8) | copy-start | bytes 196
  27.9 77.1 %copy-start.2 = (s32[2]{0:T(128)S(1)}, s32[2]{0:T(128)}, u32[]{:S(2)}) copy-start(s32[2]{0:T(128)} %param.7) | copy-start | bytes 28
  27.9 101.2 %copy-start.1 = (bf16[1,64,384]{2,1,0:T(8,128)(2,1)S(1)}, bf16[1,64,384]{2,1,0:T(8,128)(2,1)}, u32[]{:S(2)}) copy-start(bf16[1,64,384]{2,1,0:T(8,128)(2,1)} %param.6) | copy-start | bytes 147460
  27.9 1.4 %copy-start = (bf16[32,64,384]{2,1,0:T(8,128)(2,1)S(1)}, bf16[32,64,384]{2,1,0:T(8,128)(2,1)}, u32[]{:S(2)}) copy-start(bf16[32,64,384]{2,1,0:T(8,128)(2,1)} %get-tuple-element.87) | copy-start | bytes 4718596 | tf_op jit(solution)/shard_map/while
  45.1 1.4 %copy-start = (bf16[32,64,384]{2,1,0:T(8,128)(2,1)S(1)}, bf16[32,64,384]{2,1,0:T(8,128)(2,1)}, u32[]{:S(2)}) copy-start(bf16[32,64,384]{2,1,0:T(8,128)(2,1)} %get-tuple-element.87) | copy-start | bytes 4718596 | tf_op jit(solution)/shard_map/while
  62.2 1.4 %copy-start = (bf16[32,64,384]{2,1,0:T(8,128)(2,1)S(1)}, bf16[32,64,384]{2,1,0:T(8,128)(2,1)}, u32[]{:S(2)}) copy-start(bf16[32,64,384]{2,1,0:T(8,128)(2,1)} %get-tuple-element.87) | copy-start | bytes 4718596 | tf_op jit(solution)/shard_map/while
  79.4 1.4 %copy-start = (bf16[32,64,384]{2,1,0:T(8,128)(2,1)S(1)}, bf16[32,64,384]{2,1,0:T(8,128)(2,1)}, u32[]{:S(2)}) copy-start(bf16[32,64,384]{2,1,0:T(8,128)(2,1)} %get-tuple-element.87) | copy-start | bytes 4718596 | tf_op jit(solution)/shard_map/while
  97.2 9.8 %all-to-all-start = ((f32[16,1,1]{2,1,0:T(1,128)}), f32[16,1,1]{2,1,0:T(1,128)S(1)}, u32[]{:S(2)}, u32[]{:S(2)}) async-start(f32[16,1,1]{2,1,0:T(1,128)} %all_to_all.27), calls=%async_computation | async-start | bytes 16384 | tf_op jit(solution)/shard_map/all_to_all | solution.py:70
  107.0 13.8 %all-to-all-start.1 = ((f32[16,1,32]{2,1,0:T(1,128)}), f32[16,1,32]{2,1,0:T(1,128)S(1)}, u32[]{:S(2)}, u32[]{:S(2)}) async-start(f32[16,1,32]{2,1,0:T(1,128)} %bitcast.10), calls=%async_computation.1 | async-start | bytes 16384 | tf_op jit(solution)/shard_map/all_to_all | solution.py:69
  112.3 5.7 %collective-permute-start.2 = (f32[1]{0:T(128)}, f32[1]{0:T(128)}, u32[]{:S(2)}, u32[]{:S(2)}) collective-permute-start(f32[1]{0:T(128)} %bitcast.7), channel_id=1, source_target_pairs={{0,1},{1,2},{2,3},{3,4},{4,5},{5,6},{6,7},{7,8},{8,9},{9,10},{10,1... | collective-permute-start | bytes 20 | tf_op jit(solution)/shard_map/ppermute | solution.py:13
  112.7 5.5 %collective-permute-start.3 = (f32[1]{0:T(128)}, f32[1]{0:T(128)}, u32[]{:S(2)}, u32[]{:S(2)}) collective-permute-start(f32[1]{0:T(128)} %bitcast.7), channel_id=1, source_target_pairs={{1,0},{2,1},{3,2},{4,3},{5,4},{6,5},{7,6},{8,7},{9,8},{10,9},{11,1... | collective-permute-start | bytes 20 | tf_op jit(solution)/shard_map/ppermute | solution.py:16
  122.1 5.7 %collective-permute-start.4 = (f32[1,512]{1,0:T(1,128)S(1)}, f32[1,512]{1,0:T(1,128)S(1)}, u32[]{:S(2)}, u32[]{:S(2)}) collective-permute-start(f32[1,512]{1,0:T(1,128)S(1)} %all_to_all.26), channel_id=1, source_target_pairs={{0,1},{1,2},{2,3},{3,4},{4,5},{5,6},{6,7},{7,8},{8,9},{9,10},{10,1... | collective-permute-start | bytes 6152 | tf_op jit(solution)/shard_map/ppermute | solution.py:13
  122.1 5.7 %collective-permute-start.5 = (f32[1,512]{1,0:T(1,128)S(1)}, f32[1,512]{1,0:T(1,128)S(1)}, u32[]{:S(2)}, u32[]{:S(2)}) collective-permute-start(f32[1,512]{1,0:T(1,128)S(1)} %all_to_all.26), channel_id=1, source_target_pairs={{1,0},{2,1},{3,2},{4,3},{5,4},{6,5},{7,6},{8,7},{9,8},{10,9},{11,1... | collective-permute-start | bytes 6152 | tf_op jit(solution)/shard_map/ppermute | solution.py:16
where the time goes:
time: 131 us; the launch traced here: 130 us
  local copies, waits for them, and re-layouts  36.5 us (28%)
  other arithmetic  25 us (19%)
  starting transfers between devices  22.6 us (17%)
  blocking collectives  21.7 us (17%)
  matrix products  20.8 us (16%)
  waiting for transfers between devices  2.86 us (2%)
    dot_general x4, local copies, waits for them, and re-layouts, group_energy(): lax.dot_general(stacked, spread, batch_dims, preferred_element_type=jnp.f...  22.6 us
    all_gather x1, blocking collectives, body(): block_in = lax.all_gather(greens, 'walk', axis=0, tiled=True)  21.7 us
    reduce_sum x8, other arithmetic, group_energy(): jnp.sum((forward * mirrored).reshape(members, -1), axis=1)  18.5 us
    dot_general x4, matrix products, group_energy(): lax.dot_general(stacked, spread, batch_dims, preferred_element_type=jnp.f...  17.1 us
    ppermute x3, starting transfers between devices, padded(): lax.ppermute(lax.slice_in_dim(block, 0, width, axis=dim), axis, backward)  13.5 us
    all_to_all x1, starting transfers between devices, body(): lax.all_to_all(biases, 'walk', split_axis=0, concat_axis=1, tiled=True)  4.71 us
    broadcast_in_dim x8, local copies, waits for them, and re-layouts, group_energy(): jnp.broadcast_to(group_in[:, None], (members, chol_dev, occupied, orbitals))  4.26 us
    broadcast_in_dim x4, local copies, waits for them, and re-layouts, group_energy(): jnp.broadcast_to(cholesky[None], (members, chol_dev, occupied, orbitals))  4.15 us
  transfers between devices with their start and end apart: 8, of which 4 were waited for; matrix products, arithmetic and copies ran while one was open for 61% of the time, Pallas kernels for 0%

commit v1 on v0

v1 whole, which is shorter than its diff:
```python
import functools

import jax
import jax.numpy as jnp
from jax import lax
from jax.experimental import pallas as pl
from jax.experimental.pallas import tpu as pltpu
from jax.sharding import PartitionSpec as P

ROWS = (((1,), (1,)), ((), ()))
LANES = 128
SUB = 8


def rows_dot(a, b):
    return lax.dot_general(a, b, ROWS, preferred_element_type=jnp.float32)


def interleaved(first, second, start, count):
    return jnp.concatenate([r[start + i] for i in range(count) for r in (first, second)], axis=0)


def fold(x):
    return jnp.sum(x.reshape(x.shape[0] // SUB, SUB, x.shape[1]), axis=0)


def block_sums(ga, gb, ca, cb, sums, width):
    pairs, occ, orb = ga.shape
    half = ca.shape[0]
    tile = 2 * occ
    lane = lax.broadcasted_iota(jnp.int32, (occ, tile), 1)
    row = lax.broadcasted_iota(jnp.int32, (occ, tile), 0)
    low = lane < occ
    eye = (lane == row) | (lane - occ == row)
    sums[2 * half :, :] = jnp.zeros((SUB, pairs * tile), jnp.float32)
    step_w = min(pairs, width)

    def chunk(k, _):
        start = pl.multiple_of(k * SUB, SUB)
        for w in range(0, pairs, step_w):
            traces = [[[] for _ in range(step_w)] for _ in range(2)]
            energy = [jnp.zeros((SUB, tile), jnp.float32) for _ in range(step_w)]
            for part in range(0, SUB, 4):
                at = start + part
                ce = ca[pl.ds(at, 4)].reshape(4 * occ, orb)
                co = cb[pl.ds(at, 4)].reshape(4 * occ, orb)
                ge = ga[w : w + step_w].reshape(step_w * occ, orb)
                go = gb[w : w + step_w].reshape(step_w * occ, orb)
                fe = rows_dot(ce, interleaved(ga, gb, w, step_w))
                fo = rows_dot(co, interleaved(gb, ga, w, step_w))
                me = rows_dot(ge, interleaved(ca, cb, at, 4))
                mo = rows_dot(go, interleaved(cb, ca, at, 4))
                for j in range(step_w):
                    cols = slice(j * tile, (j + 1) * tile)
                    rows_w = slice(j * occ, (j + 1) * occ)
                    odd = jnp.zeros((SUB, tile), jnp.float32)
                    for i in range(4):
                        rows_g = slice(i * occ, (i + 1) * occ)
                        cols_g = slice(i * tile, (i + 1) * tile)
                        f0, f1 = fe[rows_g, cols], fo[rows_g, cols]
                        m0, m1 = me[rows_w, cols_g], mo[rows_w, cols_g]
                        energy[j] += fold(f0 * jnp.where(low, m0, m1))
                        odd += fold(f1 * jnp.where(low, m1, m0))
                        traces[0][j].append(jnp.sum(fold(jnp.where(eye, f0, 0.0)), axis=0, keepdims=True))
                        traces[1][j].append(jnp.sum(fold(jnp.where(eye, f1, 0.0)), axis=0, keepdims=True))
                    energy[j] += pltpu.roll(odd, occ, 1)
            for j in range(step_w):
                cols = slice((w + j) * tile, (w + j + 1) * tile)
                sums[pl.ds(start, SUB), cols] = jnp.concatenate(traces[0][j], axis=0)
                odd = jnp.concatenate(traces[1][j], axis=0)
                sums[pl.ds(half + start, SUB), cols] = pltpu.roll(odd, occ, 1)
                sums[2 * half :, cols] += energy[j]
        return 0

    lax.fori_loop(0, half // SUB, chunk, 0)


def walker_rows(sums, occ):
    columns, lanes = sums.shape
    walkers = lanes // occ
    block = lax.broadcasted_iota(jnp.int32, (walkers, lanes), 1) // occ
    owner = lax.broadcasted_iota(jnp.int32, (walkers, lanes), 0)
    ones = (block == owner).astype(jnp.bfloat16)
    total = jnp.zeros((walkers, columns), jnp.float32)
    rest = sums
    for _ in range(3):
        part = rest.astype(jnp.bfloat16)
        total += rows_dot(ones, part)
        rest = rest - part.astype(jnp.float32)
    return total


def work_kernel(source, counts, greens, chol, relocated, sent, sums):
    walkers, occ, orb = greens.shape
    me = lax.axis_index("walk")
    slots = relocated.shape[0]
    live = counts[me]
    for t in range(slots):
        relocated[t] = jnp.where(t < live, greens[source[t]], jnp.zeros((), jnp.bfloat16))
    half = walkers // 2
    hc = chol.shape[0] // 2
    block_sums(greens.at[:half], greens.at[half:], chol.at[:hc], chol.at[hc:], sums, 4)
    rows = walker_rows(sums[...], occ)
    for lane in range(walkers):
        w = (lane // 2) + (lane % 2) * half
        row = rows[lane : lane + 1]
        for near in range(3):
            sent[(w + 1 - near) % walkers, near : near + 1, 0 : row.shape[1]] = row


def final_kernel(scale, source, counts, got, energy, bias):
    devices = got.shape[0]
    me = lax.axis_index("walk")
    slots = bias.shape[0]
    per = bias.shape[1] // devices
    live = counts[me]
    for t in range(slots):
        near = lax.rem(source[t] - me + 1 + devices, devices)
        rows = jnp.where(near == 0, got[:, 0, :], jnp.where(near == 1, got[:, 1, :], got[:, 2, :]))
        rows = jnp.where(t < live, rows, 0.0)
        bias[t : t + 1, :] = jnp.concatenate([rows[d : d + 1, :per] for d in range(devices)], axis=1)
        total = jnp.sum(rows[:, per : per + SUB])
        energy[t : t + 1, :] = jnp.full((1, LANES), total * scale)


def body(greens, source, counts, cholesky):
    devices = lax.axis_size("walk")
    chol_dev, occ, orb = cholesky.shape
    slots = source.shape[0]
    nchol = chol_dev * devices
    vmem = pl.BlockSpec(memory_space=pltpu.VMEM)
    smem = pl.BlockSpec(memory_space=pltpu.SMEM)
    params = pltpu.CompilerParams(vmem_limit_bytes=48 * 2**20)
    everyone = lax.all_gather(greens, "walk", axis=0, tiled=True)
    walkers = everyone.shape[0]
    relocated, sent = pl.pallas_call(
        work_kernel,
        out_shape=(
            jax.ShapeDtypeStruct((slots, occ, orb), jnp.bfloat16),
            jax.ShapeDtypeStruct((devices, 3, LANES), jnp.float32),
        ),
        in_specs=[smem, smem, vmem, vmem],
        out_specs=[vmem, vmem],
        scratch_shapes=[pltpu.VMEM((chol_dev + SUB, walkers * occ), jnp.float32)],
        compiler_params=params,
    )(source, counts, everyone, cholesky)
    got = lax.all_to_all(sent, "walk", split_axis=0, concat_axis=0, tiled=True)
    energy, bias = pl.pallas_call(
        functools.partial(final_kernel, -(0.5 / nchol)),
        out_shape=(
            jax.ShapeDtypeStruct((slots, LANES), jnp.float32),
            jax.ShapeDtypeStruct((slots, nchol), jnp.float32),
        ),
        in_specs=[smem, smem, vmem],
        out_specs=[vmem, vmem],
        compiler_params=params,
    )(source, counts, got)
    return relocated, energy[:, 0], bias


def solution(mesh):
    return jax.shard_map(
        body,
        mesh=mesh,
        in_specs=(
            P(("rep", "walk"), None, None),
            P(("rep", "walk")),
            P("rep"),
            P("walk", None, None),
        ),
        out_specs=(P(("rep", "walk"), None, None), P(("rep", "walk")), P(("rep", "walk"), None)),
        check_vma=False,
    )
```

time: 131 us -> 46.8 us (0.36)
  local copies, waits for them, and re-layouts: 36.5 us -> 3.34 us
  other arithmetic: 25 us -> 0 us
  starting transfers between devices: 22.6 us -> 0 us
  matrix products: 20.8 us -> 0 us
  blocking collectives: 21.7 us -> 34.9 us
  Pallas kernels: 0 us -> 7.72 us
  waiting for transfers between devices: 2.86 us -> 0 us
    dot_general x4 -> x0, local copies, waits for them, and re-layouts: 22.6 us -> none  [group_energy(): lax.dot_general(stacked, spread, batch_dims, preferred_element_type=jnp.f...]
    dot_general x5 -> x0, matrix products: 20.8 us -> none  [the longest x4 17.1 us: group_energy(): lax.dot_general(stacked, spread, batch_dims, preferred_element_type=jnp.f...]
    reduce_sum x9 -> x0, other arithmetic: 19.1 us -> none  [the longest x8 18.5 us: group_energy(): jnp.sum((forward * mirrored).reshape(members, -1), axis=1)]
    ppermute x6 -> x0, starting transfers between devices: 14.5 us -> none  [the longest x3 13.5 us: padded(): lax.ppermute(lax.slice_in_dim(block, 0, width, axis=dim), axis, backward)]
    all_to_all x0 -> x1, blocking collectives: none -> 9.19 us  [body(): got = lax.all_to_all(sent, 'walk', split_axis=0, concat_axis=0, tiled=True)]
    broadcast_in_dim x12 -> x0, local copies, waits for them, and re-layouts: 8.41 us -> none  [the longest x8 4.26 us: group_energy(): jnp.broadcast_to(group_in[:, None], (members, chol_dev, occupied, orbitals))]
    all_to_all x2 -> x0, starting transfers between devices: 8.18 us -> none  [the longest x1 4.71 us: body(): lax.all_to_all(biases, 'walk', split_axis=0, concat_axis=1, tiled=True)]
    pallas_call x0 -> x2, Pallas kernels: none -> 7.72 us  [the longest x1 6.38 us: body(): pl.pallas_call(work_kernel, out_shape=(jax.ShapeDtypeStruct((slots, occ,...]
  transfers between devices with their start and end apart: 8 -> 0, of which waited for: 4 -> 0; matrix products, arithmetic and copies ran while one was open for 61% -> 0% of each run, Pallas kernels for 0% -> 0%
where the time goes in v1:
time: 46.8 us; the launch traced here: 46.6 us
  blocking collectives  34.9 us (75%)
  Pallas kernels  7.72 us (16%)
  local copies, waits for them, and re-layouts  3.34 us (7%)
  between operations  0.63 us (1%)
    all_gather x1, blocking collectives, body(): everyone = lax.all_gather(greens, 'walk', axis=0, tiled=True)  25.7 us
    all_to_all x1, blocking collectives, body(): got = lax.all_to_all(sent, 'walk', split_axis=0, concat_axis=0, tiled=True)  9.19 us
    pallas_call x1, Pallas kernels, body(): pl.pallas_call(work_kernel, out_shape=(jax.ShapeDtypeStruct((slots, occ,...  6.38 us
    unnamed x6, local copies, waits for them, and re-layouts  2.72 us
    pallas_call x1, Pallas kernels, body(): pl.pallas_call(functools.partial(final_kernel, -(0.5 / nchol)), out_shape...  1.34 us

profile of v1, /device:TPU:0, one launch (start us, length us, event | category | flops | bytes accessed | tf_op | source)
XLA Modules:
  0.0 46.6 jit_solution(12842531558102504623)
XLA Ops:
  0.6 25.7 %all_gather.3.greens = bf16[16,64,384]{2,1,0:T(8,128)(2,1)S(1)} all-gather(bf16[1,64,384]{2,1,0:T(8,128)(2,1)} %param.4), channel_id=1, replica_groups=mesh['rep'=2,'walk'=16] {'walk'}, dimensions={0}, use_global_device_ids=true | all-gather | bytes 835584 | tf_op jit(solution)/shard_map/all_gather | solution.py:134
  26.3 0.0 copy-start
  26.3 1.4 %copy-done = bf16[32,64,384]{2,1,0:T(8,128)(2,1)S(1)} copy-done((bf16[32,64,384]{2,1,0:T(8,128)(2,1)S(1)}, bf16[32,64,384]{2,1,0:T(8,128)(2,1)}, u32[]{:S(2)}) %copy-start) | copy-done | bytes 1572888
  27.8 0.0 copy-start.1
  27.8 0.7 %copy-done.1 = s32[2]{0:T(128)S(1)} copy-done((s32[2]{0:T(128)S(1)}, s32[2]{0:T(128)}, u32[]{:S(2)}) %copy-start.1) | copy-done | bytes 32
  28.4 0.0 copy-start.2
  28.4 0.7 %copy-done.2 = s32[16]{0:T(128)S(1)} copy-done((s32[16]{0:T(128)S(1)}, s32[16]{0:T(128)}, u32[]{:S(2)}) %copy-start.2) | copy-done | bytes 88
  29.1 6.4 %shard_map.67 = (bf16[2,64,384]{2,1,0:T(8,128)(2,1)}, f32[16,3,128]{2,1,0:T(4,128)S(1)}) custom-call(s32[2]{0:T(128)S(1)} %copy-done.1, s32[16]{0:T(128)S(1)} %copy-done.2, bf16[16,64,384]{2,1,0:T(8,128)(2,1)S(1)} %all_gather.3.greens, bf16[32,64,384]{2,1,0:T(8,128)(2,1)S(1)} %copy-done), custom_call_target="tpu_custom_call" | custom-call | tf_op jit(solution)/shard_map/pallas_call | solution.py:136
  35.4 9.2 %all_to_all.5.got = f32[16,3,128]{2,1,0:T(4,128)S(1)} all-to-all(f32[16,3,128]{2,1,0:T(4,128)S(1)} %get-tuple-element.8), channel_id=1, replica_groups=mesh['rep'=2,'walk'=16] {'walk'}, dimensions={0} | all-to-all | bytes 49152 | tf_op jit(solution)/shard_map/all_to_all | solution.py:147
  44.6 1.3 %shard_map.68 = (f32[2,128]{1,0:T(2,128)S(1)}, f32[2,512]{1,0:T(2,128)}) custom-call(s32[2]{0:T(128)S(1)} %copy-done.1, s32[16]{0:T(128)S(1)} %copy-done.2, f32[16,3,128]{2,1,0:T(4,128)S(1)} %all_to_all.5.got), custom_call_target="tpu_custom_call" | custom-call | tf_op jit(solution)/shard_map/pallas_call | solution.py:148
  46.0 0.6 %slice_reduce_fusion = f32[2]{0:T(128)} fusion(f32[2,128]{1,0:T(2,128)S(1)} %get-tuple-element.9), kind=kLoop, calls=%fused_computation | loop fusion | bytes 16 | tf_op jit(solution)/shard_map/slice | solution.py:158
Async XLA Ops:
  26.3 1.4 %copy-start = (bf16[32,64,384]{2,1,0:T(8,128)(2,1)S(1)}, bf16[32,64,384]{2,1,0:T(8,128)(2,1)}, u32[]{:S(2)}) copy-start(bf16[32,64,384]{2,1,0:T(8,128)(2,1)} %chol.1) | copy-start | bytes 4718596
  27.8 0.7 %copy-start.1 = (s32[2]{0:T(128)S(1)}, s32[2]{0:T(128)}, u32[]{:S(2)}) copy-start(s32[2]{0:T(128)} %source.3) | copy-start | bytes 28
  28.4 0.7 %copy-start.2 = (s32[16]{0:T(128)S(1)}, s32[16]{0:T(128)}, u32[]{:S(2)}) copy-start(s32[16]{0:T(128)} %counts.3) | copy-start | bytes 196

commit v2 on v1

v2 whole, which is shorter than its diff:
```python
import functools

import jax
import jax.numpy as jnp
from jax import lax
from jax.experimental import pallas as pl
from jax.experimental.pallas import tpu as pltpu
from jax.sharding import PartitionSpec as P

ROWS = (((1,), (1,)), ((), ()))
LANES = 128
SUB = 8
NEAR = 3
STEP = 8


def rows_dot(a, b):
    return lax.dot_general(a, b, ROWS, preferred_element_type=jnp.float32)


def fold(x):
    return jnp.sum(x.reshape(x.shape[0] // SUB, SUB, x.shape[1]), axis=0)


def block_sums(blocks, ca, cb, sums, side, core):
    _, occ, orb = blocks[0].shape
    half = ca.shape[0]
    tile = 2 * occ
    lane = lax.broadcasted_iota(jnp.int32, (occ, tile), 1)
    row = lax.broadcasted_iota(jnp.int32, (occ, tile), 0)
    low = lane < occ
    eye = (lane == row) | (lane - occ == row)
    count = len(blocks)
    walkers = [jnp.concatenate(blocks[j : j + 2], axis=0).reshape(-1, orb) for j in range(0, count, 2)]
    spare = pl.ds(pl.multiple_of((1 - side) * 2 * half, 2 * half), 2 * half)
    sums[spare, :] = jnp.zeros((2 * half, count * tile), jnp.float32)

    def chunk(k, energies):
        energies = list(energies)
        start = pl.multiple_of(k * STEP, STEP)
        va = ca[pl.ds(start, STEP)].reshape(STEP * occ, orb)
        vb = cb[pl.ds(start, STEP)].reshape(STEP * occ, orb)
        for j in range(count):
            if j % 2 == 0:
                fa = rows_dot(va, walkers[j // 2])
                fb = rows_dot(vb, walkers[j // 2])
            cols = slice((j % 2) * tile, (j % 2 + 1) * tile)
            traces = [[], []]
            for i in range(STEP):
                rows = slice(i * occ, (i + 1) * occ)
                f0, f1 = fa[rows, cols], fb[rows, cols]
                turned = jnp.transpose(jnp.concatenate([f0, f1], axis=0))
                t0, t1 = turned[:occ], turned[occ:]
                crossed = pltpu.roll(jnp.where(low, t1, t0), occ, 1)
                energies[j] += fold(f0 * jnp.where(low, t0, crossed) + f1 * jnp.where(low, crossed, t1))
                for part, f in enumerate((f0, f1)):
                    traces[part].append(jnp.sum(fold(jnp.where(eye, f, 0.0)), axis=0, keepdims=True))
            for part in range(2):
                at = (2 * side + jnp.where(core == 0, part, 1 - part)) * half + start
                at = pl.ds(pl.multiple_of(at, STEP), STEP)
                sums[at, j * tile : (j + 1) * tile] = jnp.concatenate(traces[part], axis=0)
        return tuple(energies)

    zero = jnp.zeros((SUB, tile), jnp.float32)
    steps = half // STEP
    energies = lax.fori_loop(0, steps, chunk, (zero,) * count, unroll=steps if count <= 4 else 1)
    spare = pl.ds(pl.multiple_of((1 - side) * 2 * half, SUB), SUB)
    for j in range(count):
        sums[spare, j * tile : (j + 1) * tile] = energies[j]


def walker_rows(sums, occ):
    rows, lanes = sums.shape
    walkers = lanes // occ
    block = lax.broadcasted_iota(jnp.int32, (walkers, lanes), 1) // occ
    owner = lax.broadcasted_iota(jnp.int32, (walkers, lanes), 0)
    ones = (block == owner).astype(jnp.bfloat16)
    parts = []
    for _ in range(3):
        parts.append(sums.astype(jnp.bfloat16))
        sums = sums - parts[-1].astype(jnp.float32)
    total = rows_dot(ones, jnp.concatenate(parts, axis=0))
    return total[:, :rows] + total[:, rows : 2 * rows] + total[:, 2 * rows :]


def own_kernel(greens, partner, own):
    own[0] = greens[0]
    own[1] = partner[0]


def early_kernel(own, cross, block, mine, other, sums):
    me = lax.axis_index("walk")
    chip, core = me // 2, me % 2
    values = [jnp.concatenate([own[0:1], cross[...]], axis=0)] + [b[...] for b in block]
    block_sums(values, mine, other, sums, chip % 2, core)


def late_kernel(odds, far, half, forwarded, ca, cb, early, sent, sums):
    devices = sent.shape[0]
    occ = far.shape[1]
    me = lax.axis_index("walk")
    chip, core = me // 2, me % 2
    values = [jnp.concatenate([half[...], forwarded[...]], axis=0), far[...]]
    block_sums(values, ca, cb, sums, chip % 2, core)
    rows = walker_rows(jnp.concatenate([early[...], sums[...]], axis=1), occ)
    sent[...] = jnp.zeros_like(sent)
    plain = core == chip % 2
    walkers = [me, 2 * (chip ^ 1) + 1 - core]
    for s in odds:
        if s == 5:
            walkers += [me ^ 8, me ^ 10]
        else:
            there = chip ^ jnp.where(plain, s, s - 1)
            lead = jnp.where(plain, core, 1 - core)
            walkers += [2 * there + lead, 2 * there + 1 - lead]
    for r, walker in enumerate(walkers):
        for near in range(NEAR):
            sent[lax.rem(walker + 1 - near + devices, devices), near : near + 1, :] = rows[r : r + 1]


def relocate_kernel(shifts, source, counts, own, cross, *refs):
    blocks, (relocated, pick) = refs[:-2], refs[-2:]
    me = lax.axis_index("walk")
    chip, core = me // 2, me % 2
    devices = counts.shape[0]
    chips = devices // 2
    shift = chip ^ lax.rem(chip + jnp.where(core == 0, chips - 1, 1), chips)
    outer = cross[0]
    for s, block in zip(shifts, blocks):
        outer = jnp.where(shift == s, block[1], outer)
    row = lax.broadcasted_iota(jnp.int32, pick.shape[1:], 0)
    for t in range(relocated.shape[0]):
        near = lax.rem(source[t] - me + 1 + devices, devices)
        value = jnp.where(near == 1, own[0], jnp.where(near == 2 * core, outer, own[1]))
        relocated[t] = jnp.where(t < counts[me], value, jnp.zeros((), jnp.bfloat16))
        pick[t] = jnp.where((row == near) & (t < counts[me]), 1.0, 0.0)


def final_kernel(scale, pick, got, energy, bias):
    devices = got.shape[0]
    low = lax.broadcasted_iota(jnp.int32, pick.shape[1:], 1) < LANES // 2
    parts = jnp.zeros(pick.shape[1:], jnp.float32)
    for q in range(devices // 4):
        even = got[4 * q] + got[4 * q + 1]
        odd = got[4 * q + 2] + got[4 * q + 3]
        tile = jnp.where(low, even, odd)
        parts += jnp.where(low, odd, even)
        for t in range(bias.shape[0]):
            bias[t : t + 1, q * LANES : (q + 1) * LANES] = jnp.sum(tile * pick[t], axis=0, keepdims=True)
    for t in range(bias.shape[0]):
        energy[t] = jnp.sum(parts * pick[t]) * scale


def body(greens, source, counts, cholesky):
    devices = lax.axis_size("walk")
    chips = devices // 2
    chol_dev, occ, orb = cholesky.shape
    slots = source.shape[0]
    nchol = chol_dev * devices
    assert greens.shape[0] == 1 and 4 * chol_dev == LANES and 2 * occ == LANES
    assert chips >= 8 and chips & (chips - 1) == 0
    vmem = pl.BlockSpec(memory_space=pltpu.VMEM)
    smem = pl.BlockSpec(memory_space=pltpu.SMEM)
    params = pltpu.CompilerParams(vmem_limit_bytes=20 * 2**20)

    def permuted(x, source_of):
        return lax.ppermute(x, "walk", [(2 * n + k, 2 * m + c) for m in range(chips) for c in range(2) for n, k in [source_of(m, c)]])

    def trade(s):
        return permuted(own, lambda m, c: (m ^ s, c) if c == m % 2 else (m ^ (s - 1), 1 - c))

    partner = permuted(greens, lambda m, c: (m, 1 - c))
    half = permuted(greens, lambda m, c: (m ^ 4, c))
    cross = permuted(greens, lambda m, c: (m ^ 1, 1 - c))
    own = pl.pallas_call(
        own_kernel,
        out_shape=jax.ShapeDtypeStruct((2, occ, orb), greens.dtype),
        in_specs=[vmem, vmem],
        out_specs=vmem,
        compiler_params=params,
        cost_estimate=pl.CostEstimate(flops=4 * 10**9, bytes_accessed=4 * occ * orb, transcendentals=0),
    )(greens, partner)
    after_own, own = lax.optimization_barrier((cholesky, own))
    other = permuted(after_own, lambda m, c: (m, 1 - c))
    far = trade(7)
    beside = [trade(s) for s in [3] + list(range(9, chips, 2))]
    forwarded = permuted(half, lambda m, c: (m ^ 1, c))
    held = dict(zip([3] + list(range(9, chips, 2)) + [7], beside + [far]))
    odds = [3] + list(range(9, chips, 2)) + [5, 7]
    shifts = [2**k - 1 for k in range(2, chips.bit_length())]
    count = 1 + len(beside)

    def cost(blocks):
        flops = 2 * (2 * blocks * occ) * (2 * chol_dev * occ) * orb
        return pl.CostEstimate(flops=flops, bytes_accessed=4 * chol_dev * occ * orb, transcendentals=0)

    early = pl.pallas_call(
        lambda own, cross, *r: early_kernel(own, cross, r[: count - 1], *r[count - 1 :]),
        out_shape=jax.ShapeDtypeStruct((LANES, 2 * count * occ), jnp.float32),
        in_specs=[vmem] * (count + 3),
        out_specs=vmem,
        compiler_params=params,
        cost_estimate=cost(count),
    )(own, cross, *beside, cholesky, other)
    sent = pl.pallas_call(
        functools.partial(late_kernel, odds),
        out_shape=jax.ShapeDtypeStruct((devices, NEAR, LANES), jnp.float32),
        in_specs=[vmem] * 6,
        out_specs=vmem,
        scratch_shapes=[pltpu.VMEM((LANES, 4 * occ), jnp.float32)],
        compiler_params=params,
        cost_estimate=cost(2),
    )(far, half, forwarded, cholesky, other, early)
    got = lax.all_to_all(sent, "walk", split_axis=0, concat_axis=0, tiled=True)
    relocated, pick = pl.pallas_call(
        functools.partial(relocate_kernel, shifts),
        out_shape=(
            jax.ShapeDtypeStruct((slots, occ, orb), jnp.bfloat16),
            jax.ShapeDtypeStruct((slots, NEAR, LANES), jnp.float32),
        ),
        in_specs=[smem, smem] + [vmem] * (2 + len(shifts)),
        out_specs=[vmem, vmem],
        compiler_params=params,
    )(source, counts, own, cross, *[held[s] for s in shifts])
    energy, force_bias = pl.pallas_call(
        functools.partial(final_kernel, -(0.5 / nchol)),
        out_shape=(
            jax.ShapeDtypeStruct((slots,), jnp.float32),
            jax.ShapeDtypeStruct((slots, nchol), jnp.float32),
        ),
        in_specs=[vmem, vmem],
        out_specs=[smem, vmem],
        compiler_params=params,
    )(pick, got)
    return relocated, energy, force_bias


def solution(mesh):
    return jax.shard_map(
        body,
        mesh=mesh,
        in_specs=(
            P(("rep", "walk"), None, None),
            P(("rep", "walk")),
            P("rep"),
            P("walk", None, None),
        ),
        out_specs=(P(("rep", "walk"), None, None), P(("rep", "walk")), P(("rep", "walk"), None)),
        check_vma=False,
    )
```

time: 46.8 us -> 34.2 us (0.73)
  blocking collectives: 34.9 us -> 0 us
  starting transfers between devices: 0 us -> 15 us
  waiting for transfers between devices: 0 us -> 10.5 us
  local copies, waits for them, and re-layouts: 3.34 us -> 0.82 us
  Pallas kernels: 7.72 us -> 6.89 us
    all_gather x1 -> x0, blocking collectives: 25.7 us -> none  [body(): everyone = lax.all_gather(greens, 'walk', axis=0, tiled=True)]
    all_to_all x1 -> x0, blocking collectives: 9.19 us -> none  [body(): got = lax.all_to_all(sent, 'walk', split_axis=0, concat_axis=0, tiled=True)]
    ppermute x0 -> x7, starting transfers between devices: none -> 8.9 us  [permuted(): lax.ppermute(x, 'walk', [(2 * n + k, 2 * m + c) for m in range(chips) for...]
    all_to_all x0 -> x1, starting transfers between devices: none -> 6.12 us  [body(): got = lax.all_to_all(sent, 'walk', split_axis=0, concat_axis=0, tiled=True)]
    all_to_all x0 -> x1, waiting for transfers between devices: none -> 5.39 us  [body(): got = lax.all_to_all(sent, 'walk', split_axis=0, concat_axis=0, tiled=True)]
    ppermute x0 -> x7, waiting for transfers between devices: none -> 5.11 us  [permuted(): lax.ppermute(x, 'walk', [(2 * n + k, 2 * m + c) for m in range(chips) for...]
    unnamed x6 -> x10, local copies, waits for them, and re-layouts: 2.72 us -> 0.82 us
    pallas_call x1, Pallas kernels: 1.34 us -> 0.65 us  [body(): pl.pallas_call(functools.partial(final_kernel, -(0.5 / nchol)), out_shape...]
  transfers between devices with their start and end apart: 0 -> 8, of which waited for: 0 -> 5; matrix products, arithmetic and copies ran while one was open for 0% -> 0% of each run, Pallas kernels for 0% -> 10%
where the time goes in v2:
time: 34.2 us; the launch traced here: 33.9 us
  starting transfers between devices  15 us (44%)
  waiting for transfers between devices  10.5 us (31%)
  Pallas kernels  6.89 us (20%)
  local copies, waits for them, and re-layouts  0.82 us (2%)
  between operations  0.71 us (2%)
    ppermute x7, starting transfers between devices, permuted(): lax.ppermute(x, 'walk', [(2 * n + k, 2 * m + c) for m in range(chips) for...  8.9 us
    all_to_all x1, starting transfers between devices, body(): got = lax.all_to_all(sent, 'walk', split_axis=0, concat_axis=0, tiled=True)  6.12 us
    all_to_all x1, waiting for transfers between devices, body(): got = lax.all_to_all(sent, 'walk', split_axis=0, concat_axis=0, tiled=True)  5.39 us
    ppermute x7, waiting for transfers between devices, permuted(): lax.ppermute(x, 'walk', [(2 * n + k, 2 * m + c) for m in range(chips) for...  5.11 us
    pallas_call x1, Pallas kernels, body(): pl.pallas_call(functools.partial(late_kernel, odds), out_shape=jax.ShapeD...  2.9 us
    pallas_call x1, Pallas kernels, body(): pl.pallas_call(lambda own, cross, *r: early_kernel(own, cross, r[:count -...  2.11 us
    pallas_call x1, Pallas kernels, body(): pl.pallas_call(functools.partial(relocate_kernel, shifts), out_shape=(jax...  1.23 us
    unnamed x10, local copies, waits for them, and re-layouts  0.82 us
  transfers between devices with their start and end apart: 8, of which 5 were waited for; matrix products, arithmetic and copies ran while one was open for 0% of the time, Pallas kernels for 10%

profile of v2, /device:TPU:0, one launch (start us, length us, event | category | flops | bytes accessed | tf_op | source)
XLA Modules:
  0.0 33.9 jit_solution(17518529789303660924)
XLA Ops:
  0.6 0.0 copy-start
  0.6 0.5 %collective-permute-start = (bf16[1,64,384]{2,1,0:T(8,128)(2,1)}, bf16[1,64,384]{2,1,0:T(8,128)(2,1)S(1)}, u32[]{:S(2)}, u32[]{:S(2)}) collective-permute-start(bf16[1,64,384]{2,1,0:T(8,128)(2,1)} %greens.1), channel_id=1, source_target_pairs={{1,0},{0,1},{3,2},{2,3},{5,4},{4,5},{7,6},{6,7},{9,8},{8,9},{11,10... | collective-permute-start | bytes 147464 | tf_op jit(solution)/shard_map/ppermute | solution.py:167
  1.2 1.1 %collective-permute-done.partner = bf16[1,64,384]{2,1,0:T(8,128)(2,1)S(1)} collective-permute-done((bf16[1,64,384]{2,1,0:T(8,128)(2,1)}, bf16[1,64,384]{2,1,0:T(8,128)(2,1)S(1)}, u32[]{:S(2)}, u32[]{:S(2)}) %collective-permute-start) | collective-permute-done | bytes 49184 | tf_op jit(solution)/shard_map/ppermute | solution.py:167
  2.2 0.0 copy-start.3
  2.3 0.8 %copy-done.3 = bf16[1,64,384]{2,1,0:T(8,128)(2,1)S(1)} copy-done((bf16[1,64,384]{2,1,0:T(8,128)(2,1)S(1)}, bf16[1,64,384]{2,1,0:T(8,128)(2,1)}, u32[]{:S(2)}) %copy-start.3) | copy-done | bytes 49176
  3.0 0.0 copy-start.4
  3.1 0.0 copy-done
  3.1 0.4 %collective-permute-start.6 = (bf16[32,64,384]{2,1,0:T(8,128)(2,1)S(1)}, bf16[32,64,384]{2,1,0:T(8,128)(2,1)S(1)}, u32[]{:S(2)}, u32[]{:S(2)}) collective-permute-start(bf16[32,64,384]{2,1,0:T(8,128)(2,1)S(1)} %copy-done), channel_id=1, source_target_pairs={{1,0},{0,1},{3,2},{2,3},{5,4},{4,5},{7,6},{6,7},{9,8},{8,9},{11,10... | collective-permute-start | bytes 4718600 | tf_op jit(solution)/shard_map/ppermute | solution.py:167
  3.5 2.7 %collective-permute-start.2 = (bf16[2,64,384]{2,1,0:T(8,128)(2,1)S(1)}, bf16[2,64,384]{2,1,0:T(8,128)(2,1)S(1)}, u32[]{:S(2)}, u32[]{:S(2)}) collective-permute-start(bf16[2,64,384]{2,1,0:T(8,128)(2,1)S(1)} %shard_map.67.own), channel_id=1, source_target_pairs={{6,0},{4,1},{7,2},{5,3},{2,4},{0,5},{3,6},{1,7},{14,8},{12,9},{15,... | collective-permute-start | bytes 294920 | tf_op jit(solution)/shard_map/ppermute | solution.py:167
  6.2 0.0 copy-done.4
  6.2 2.6 %collective-permute-start.4 = (bf16[1,64,384]{2,1,0:T(8,128)(2,1)S(1)}, bf16[1,64,384]{2,1,0:T(8,128)(2,1)S(1)}, u32[]{:S(2)}, u32[]{:S(2)}) collective-permute-start(bf16[1,64,384]{2,1,0:T(8,128)(2,1)S(1)} %copy-done.4), channel_id=1, source_target_pairs={{8,0},{9,1},{10,2},{11,3},{12,4},{13,5},{14,6},{15,7},{0,8},{1,9},... | collective-permute-start | bytes 147464 | tf_op jit(solution)/shard_map/ppermute | solution.py:167
  8.8 1.0 %collective-permute-start.1 = (bf16[1,64,384]{2,1,0:T(8,128)(2,1)S(1)}, bf16[1,64,384]{2,1,0:T(8,128)(2,1)S(1)}, u32[]{:S(2)}, u32[]{:S(2)}) collective-permute-start(bf16[1,64,384]{2,1,0:T(8,128)(2,1)S(1)} %copy-done.4), channel_id=1, source_target_pairs={{3,0},{2,1},{1,2},{0,3},{7,4},{6,5},{5,6},{4,7},{11,8},{10,9},{9,1... | collective-permute-start | bytes 147464 | tf_op jit(solution)/shard_map/ppermute | solution.py:167
  9.8 0.6 %collective-permute-start.3 = (bf16[2,64,384]{2,1,0:T(8,128)(2,1)S(1)}, bf16[2,64,384]{2,1,0:T(8,128)(2,1)S(1)}, u32[]{:S(2)}, u32[]{:S(2)}) collective-permute-start(bf16[2,64,384]{2,1,0:T(8,128)(2,1)S(1)} %shard_map.67.own), channel_id=1, source_target_pairs={{14,0},{12,1},{15,2},{13,3},{10,4},{8,5},{11,6},{9,7},{6,8},{4,9},... | collective-permute-start | bytes 294920 | tf_op jit(solution)/shard_map/ppermute | solution.py:167
  10.4 1.2 %collective-permute-done.4.half = bf16[1,64,384]{2,1,0:T(8,128)(2,1)S(1)} collective-permute-done((bf16[1,64,384]{2,1,0:T(8,128)(2,1)S(1)}, bf16[1,64,384]{2,1,0:T(8,128)(2,1)S(1)}, u32[]{:S(2)}, u32[]{:S(2)}) %collective-permute-start.4) | collective-permute-done | bytes 49184 | tf_op jit(solution)/shard_map/ppermute | solution.py:167
  11.6 1.1 %collective-permute-start.5 = (bf16[1,64,384]{2,1,0:T(8,128)(2,1)S(1)}, bf16[1,64,384]{2,1,0:T(8,128)(2,1)S(1)}, u32[]{:S(2)}, u32[]{:S(2)}) collective-permute-start(bf16[1,64,384]{2,1,0:T(8,128)(2,1)S(1)} %collective-permute-done.4.half), channel_id=1, source_target_pairs={{2,0},{3,1},{0,2},{1,3},{6,4},{7,5},{4,6},{5,7},{10,8},{11,9},{8,1... | collective-permute-start | bytes 147464 | tf_op jit(solution)/shard_map/ppermute | solution.py:167
  12.7 0.0 collective-permute-done.1.cross
  12.7 0.0 collective-permute-done.2.refs_0_.r_0_
  12.7 0.0 collective-permute-done.6.r_2_.cb
  12.7 2.1 %shard_map.69.early = f32[128,256]{1,0:T(8,128)S(1)} custom-call(bf16[2,64,384]{2,1,0:T(8,128)(2,1)S(1)} %shard_map.67.own, bf16[1,64,384]{2,1,0:T(8,128)(2,1)S(1)} %collective-permute-done.1.cross, bf16[2,64,384]{2,1,0:T(8,128)(2,1)S(1)} %collective-permute-done.2.refs_0_.r_0_, bf16[32,64,384]{2,1,0:T(8,128)(2,1)S(1)} %copy-done, ...), custom_call_target="tpu_custom_call" | custom-call | flops 805306368 | bytes 3145728 | tf_op jit(solution)/shard_map/pallas_call | solution.py:197
  14.8 0.0 copy-start.1
  14.8 0.0 copy-start.2
  14.8 0.9 %collective-permute-done.5.forwarded = bf16[1,64,384]{2,1,0:T(8,128)(2,1)S(1)} collective-permute-done((bf16[1,64,384]{2,1,0:T(8,128)(2,1)S(1)}, bf16[1,64,384]{2,1,0:T(8,128)(2,1)S(1)}, u32[]{:S(2)}, u32[]{:S(2)}) %collective-permute-start.5) | collective-permute-done | bytes 49184 | tf_op jit(solution)/shard_map/ppermute | solution.py:167
  15.7 1.9 %collective-permute-done.3.refs_1_.far = bf16[2,64,384]{2,1,0:T(8,128)(2,1)S(1)} collective-permute-done((bf16[2,64,384]{2,1,0:T(8,128)(2,1)S(1)}, bf16[2,64,384]{2,1,0:T(8,128)(2,1)S(1)}, u32[]{:S(2)}, u32[]{:S(2)}) %collective-permute-start.3) | collective-permute-done | bytes 98336 | tf_op jit(solution)/shard_map/ppermute | solution.py:167
  17.6 2.9 %shard_map.70 = f32[16,3,128]{2,1,0:T(4,128)} custom-call(bf16[2,64,384]{2,1,0:T(8,128)(2,1)S(1)} %collective-permute-done.3.refs_1_.far, bf16[1,64,384]{2,1,0:T(8,128)(2,1)S(1)} %collective-permute-done.4.half, bf16[1,64,384]{2,1,0:T(8,128)(2,1)S(1)} %collective-permute-done.5.forwarded, bf16[32,64,384]{2,1,0:T(8,128)(2,1)S(1)} %copy-done, ...), custom_call_target="tpu_custom_call" | custom-call | flops 805306368 | bytes 3145728 | tf_op jit(solution)/shard_map/pallas_call | solution.py:205
  20.5 6.1 %all-to-all-start = ((f32[16,3,128]{2,1,0:T(4,128)}), f32[16,3,128]{2,1,0:T(4,128)S(1)}, u32[]{:S(2)}, u32[]{:S(2)}) async-start(f32[16,3,128]{2,1,0:T(4,128)} %shard_map.70), calls=%async_computation | async-start | bytes 65536 | tf_op jit(solution)/shard_map/all_to_all | solution.py:214
  26.6 0.0 copy-done.1
  26.7 0.0 copy-done.2
  26.7 1.2 %shard_map.68 = (bf16[2,64,384]{2,1,0:T(8,128)(2,1)}, f32[2,3,128]{2,1,0:T(4,128)S(1)}) custom-call(s32[2]{0:T(128)S(1)} %copy-done.1, s32[16]{0:T(128)S(1)} %copy-done.2, bf16[2,64,384]{2,1,0:T(8,128)(2,1)S(1)} %shard_map.67.own, bf16[1,64,384]{2,1,0:T(8,128)(2,1)S(1)} %collective-permute-done.1.cross, ...), custom_call_target="tpu_custom_call" | custom-call | tf_op jit(solution)/shard_map/pallas_call | solution.py:215
  27.9 5.4 %all-to-all-done.got = f32[16,3,128]{2,1,0:T(4,128)S(1)} async-done(((f32[16,3,128]{2,1,0:T(4,128)}), f32[16,3,128]{2,1,0:T(4,128)S(1)}, u32[]{:S(2)}, u32[]{:S(2)}) %all-to-all-start) | async-done | bytes 24608 | tf_op jit(solution)/shard_map/all_to_all | solution.py:214
  33.3 0.6 %shard_map.71 = (f32[2]{0:T(128)}, f32[2,512]{1,0:T(2,128)}) custom-call(f32[2,3,128]{2,1,0:T(4,128)S(1)} %get-tuple-element.11.pick, f32[16,3,128]{2,1,0:T(4,128)S(1)} %all-to-all-done.got), custom_call_target="tpu_custom_call" | custom-call | tf_op jit(solution)/shard_map/pallas_call | solution.py:225
  (1 shorter events, 0.0 us)
Async XLA Ops:
  0.6 2.4 %copy-start = (bf16[32,64,384]{2,1,0:T(8,128)(2,1)S(1)}, bf16[32,64,384]{2,1,0:T(8,128)(2,1)}, u32[]{:S(2)}) copy-start(bf16[32,64,384]{2,1,0:T(8,128)(2,1)} %ca.1) | copy-start | bytes 4718596
  0.6 1.6 %collective-permute-start = (bf16[1,64,384]{2,1,0:T(8,128)(2,1)}, bf16[1,64,384]{2,1,0:T(8,128)(2,1)S(1)}, u32[]{:S(2)}, u32[]{:S(2)}) collective-permute-start(bf16[1,64,384]{2,1,0:T(8,128)(2,1)} %greens.1), channel_id=1, source_target_pairs={{1,0},{0,1},{3,2},{2,3},{5,4},{4,5},{7,6},{6,7},{9,8},{8,9},{11,10... | collective-permute-start | bytes 147464 | tf_op jit(solution)/shard_map/ppermute | solution.py:167
  2.2 0.8 %copy-start.3 = (bf16[1,64,384]{2,1,0:T(8,128)(2,1)S(1)}, bf16[1,64,384]{2,1,0:T(8,128)(2,1)}, u32[]{:S(2)}) copy-start(bf16[1,64,384]{2,1,0:T(8,128)(2,1)} %greens.1) | copy-start | bytes 147460
  3.0 3.1 %copy-start.4 = (bf16[1,64,384]{2,1,0:T(8,128)(2,1)S(1)}, bf16[1,64,384]{2,1,0:T(8,128)(2,1)}, u32[]{:S(2)}) copy-start(bf16[1,64,384]{2,1,0:T(8,128)(2,1)} %greens.1) | copy-start | bytes 147460
  3.1 9.6 %collective-permute-start.6 = (bf16[32,64,384]{2,1,0:T(8,128)(2,1)S(1)}, bf16[32,64,384]{2,1,0:T(8,128)(2,1)S(1)}, u32[]{:S(2)}, u32[]{:S(2)}) collective-permute-start(bf16[32,64,384]{2,1,0:T(8,128)(2,1)S(1)} %copy-done), channel_id=1, source_target_pairs={{1,0},{0,1},{3,2},{2,3},{5,4},{4,5},{7,6},{6,7},{9,8},{8,9},{11,10... | collective-permute-start | bytes 4718600 | tf_op jit(solution)/shard_map/ppermute | solution.py:167
  3.5 9.2 %collective-permute-start.2 = (bf16[2,64,384]{2,1,0:T(8,128)(2,1)S(1)}, bf16[2,64,384]{2,1,0:T(8,128)(2,1)S(1)}, u32[]{:S(2)}, u32[]{:S(2)}) collective-permute-start(bf16[2,64,384]{2,1,0:T(8,128)(2,1)S(1)} %shard_map.67.own), channel_id=1, source_target_pairs={{6,0},{4,1},{7,2},{5,3},{2,4},{0,5},{3,6},{1,7},{14,8},{12,9},{15,... | collective-permute-start | bytes 294920 | tf_op jit(solution)/shard_map/ppermute | solution.py:167
  6.2 5.4 %collective-permute-start.4 = (bf16[1,64,384]{2,1,0:T(8,128)(2,1)S(1)}, bf16[1,64,384]{2,1,0:T(8,128)(2,1)S(1)}, u32[]{:S(2)}, u32[]{:S(2)}) collective-permute-start(bf16[1,64,384]{2,1,0:T(8,128)(2,1)S(1)} %copy-done.4), channel_id=1, source_target_pairs={{8,0},{9,1},{10,2},{11,3},{12,4},{13,5},{14,6},{15,7},{0,8},{1,9},... | collective-permute-start | bytes 147464 | tf_op jit(solution)/shard_map/ppermute | solution.py:167
  8.8 3.9 %collective-permute-start.1 = (bf16[1,64,384]{2,1,0:T(8,128)(2,1)S(1)}, bf16[1,64,384]{2,1,0:T(8,128)(2,1)S(1)}, u32[]{:S(2)}, u32[]{:S(2)}) collective-permute-start(bf16[1,64,384]{2,1,0:T(8,128)(2,1)S(1)} %copy-done.4), channel_id=1, source_target_pairs={{3,0},{2,1},{1,2},{0,3},{7,4},{6,5},{5,6},{4,7},{11,8},{10,9},{9,1... | collective-permute-start | bytes 147464 | tf_op jit(solution)/shard_map/ppermute | solution.py:167
  9.8 7.8 %collective-permute-start.3 = (bf16[2,64,384]{2,1,0:T(8,128)(2,1)S(1)}, bf16[2,64,384]{2,1,0:T(8,128)(2,1)S(1)}, u32[]{:S(2)}, u32[]{:S(2)}) collective-permute-start(bf16[2,64,384]{2,1,0:T(8,128)(2,1)S(1)} %shard_map.67.own), channel_id=1, source_target_pairs={{14,0},{12,1},{15,2},{13,3},{10,4},{8,5},{11,6},{9,7},{6,8},{4,9},... | collective-permute-start | bytes 294920 | tf_op jit(solution)/shard_map/ppermute | solution.py:167
  11.6 4.1 %collective-permute-start.5 = (bf16[1,64,384]{2,1,0:T(8,128)(2,1)S(1)}, bf16[1,64,384]{2,1,0:T(8,128)(2,1)S(1)}, u32[]{:S(2)}, u32[]{:S(2)}) collective-permute-start(bf16[1,64,384]{2,1,0:T(8,128)(2,1)S(1)} %collective-permute-done.4.half), channel_id=1, source_target_pairs={{2,0},{3,1},{0,2},{1,3},{6,4},{7,5},{4,6},{5,7},{10,8},{11,9},{8,1... | collective-permute-start | bytes 147464 | tf_op jit(solution)/shard_map/ppermute | solution.py:167
  14.8 11.8 %copy-start.1 = (s32[2]{0:T(128)S(1)}, s32[2]{0:T(128)}, u32[]{:S(2)}) copy-start(s32[2]{0:T(128)} %source.1) | copy-start | bytes 28
  14.8 11.8 %copy-start.2 = (s32[16]{0:T(128)S(1)}, s32[16]{0:T(128)}, u32[]{:S(2)}) copy-start(s32[16]{0:T(128)} %counts.1) | copy-start | bytes 196
  20.5 12.8 %all-to-all-start = ((f32[16,3,128]{2,1,0:T(4,128)}), f32[16,3,128]{2,1,0:T(4,128)S(1)}, u32[]{:S(2)}, u32[]{:S(2)}) async-start(f32[16,3,128]{2,1,0:T(4,128)} %shard_map.70), calls=%async_computation | async-start | bytes 65536 | tf_op jit(solution)/shard_map/all_to_all | solution.py:214

commit v3 on v2

--- a/solution.py
+++ b/solution.py
@@ -88,55 +88,86 @@
     own[1] = partner[0]
 
 
-def early_kernel(own, cross, block, mine, other, sums):
+def walker_ids(odds):
     me = lax.axis_index("walk")
     chip, core = me // 2, me % 2
-    values = [jnp.concatenate([own[0:1], cross[...]], axis=0)] + [b[...] for b in block]
-    block_sums(values, mine, other, sums, chip % 2, core)
-
-
-def late_kernel(odds, far, half, forwarded, ca, cb, early, sent, sums):
+    plain = core == chip % 2
+    ids = []
+    for s in odds:
+        there = chip ^ jnp.where(plain, s, s - 1)
+        lead = jnp.where(plain, core, 1 - core)
+        ids += [2 * there + lead, 2 * there + 1 - lead]
+    return ids
+
+
+def send(sent, rows, ids):
     devices = sent.shape[0]
-    occ = far.shape[1]
-    me = lax.axis_index("walk")
-    chip, core = me // 2, me % 2
-    values = [jnp.concatenate([half[...], forwarded[...]], axis=0), far[...]]
-    block_sums(values, ca, cb, sums, chip % 2, core)
-    rows = walker_rows(jnp.concatenate([early[...], sums[...]], axis=1), occ)
-    sent[...] = jnp.zeros_like(sent)
-    plain = core == chip % 2
-    walkers = [me, 2 * (chip ^ 1) + 1 - core]
-    for s in odds:
-        if s == 5:
-            walkers += [me ^ 8, me ^ 10]
-        else:
-            there = chip ^ jnp.where(plain, s, s - 1)
-            lead = jnp.where(plain, core, 1 - core)
-            walkers += [2 * there + lead, 2 * there + 1 - lead]
-    for r, walker in enumerate(walkers):
+    for r, walker in enumerate(ids):
         for near in range(NEAR):
             sent[lax.rem(walker + 1 - near + devices, devices), near : near + 1, :] = rows[r : r + 1]
 
 
-def relocate_kernel(shifts, source, counts, own, cross, *refs):
-    blocks, (relocated, pick) = refs[:-2], refs[-2:]
+def early_kernel(odds, own, cross, *refs):
+    blocks, (mine, other, blank, sent, sums) = refs[:-5], refs[-5:]
     me = lax.axis_index("walk")
     chip, core = me // 2, me % 2
+    values = [jnp.concatenate([own[0:1], cross[...]], axis=0)] + [b[...] for b in blocks]
+    block_sums(values, mine, other, sums, chip % 2, core)
+    sent[...] = blank[...]
+    rows = walker_rows(sums[...], own.shape[1])
+    send(sent, rows, [me, 2 * (chip ^ 1) + 1 - core] + walker_ids(odds))
+
+
+def next_kernel(block, mine, other, sums):
+    me = lax.axis_index("walk")
+    block_sums([block[...]], mine, other, sums, (me // 2) % 2, me % 2)
+
+
+def late_kernel(odds, *refs):
+    blocks, (mine, other, early, sent, sums) = refs[:-5], refs[-5:]
+    me = lax.axis_index("walk")
+    block_sums([b[...] for b in blocks], mine, other, sums, (me // 2) % 2, me % 2)
+    sent[...] = early[...]
+    send(sent, walker_rows(sums[...], blocks[0].shape[1]), walker_ids(odds))
+
+
+def blank_kernel(sent):
+    sent[...] = jnp.zeros_like(sent)
+
+
+def pick_kernel(source, counts, pick):
+    me = lax.axis_index("walk")
     devices = counts.shape[0]
-    chips = devices // 2
+    row = lax.broadcasted_iota(jnp.int32, pick.shape[1:], 0)
+    for t in range(pick.shape[0]):
+        near = lax.rem(source[t] - me + 1 + devices, devices)
+        pick[t] = jnp.where((row == near) & (t < counts[me]), 1.0, 0.0)
+
+
+def relocate(shifts, pick, own, cross, blocks, relocated):
+    me = lax.axis_index("walk")
+    chip, core = me // 2, me % 2
+    chips = lax.axis_size("walk") // 2
     shift = chip ^ lax.rem(chip + jnp.where(core == 0, chips - 1, 1), chips)
     outer = cross[0]
     for s, block in zip(shifts, blocks):
         outer = jnp.where(shift == s, block[1], outer)
-    row = lax.broadcasted_iota(jnp.int32, pick.shape[1:], 0)
+    before, after = jnp.where(core == 0, outer, own[1]), jnp.where(core == 0, own[1], outer)
     for t in range(relocated.shape[0]):
-        near = lax.rem(source[t] - me + 1 + devices, devices)
-        value = jnp.where(near == 1, own[0], jnp.where(near == 2 * core, outer, own[1]))
-        relocated[t] = jnp.where(t < counts[me], value, jnp.zeros((), jnp.bfloat16))
-        pick[t] = jnp.where((row == near) & (t < counts[me]), 1.0, 0.0)
-
-
-def final_kernel(scale, pick, got, energy, bias):
+        value = jnp.zeros(relocated.shape[1:], jnp.float32)
+        for near, walker in enumerate((before, own[0], after)):
+            weight = jnp.concatenate([pick[t, near : near + 1]] * (relocated.shape[2] // LANES), axis=1)
+            value = jnp.where(weight > 0, walker.astype(jnp.float32), value)
+        relocated[t] = value.astype(relocated.dtype)
+
+
+def relocate_kernel(shifts, pick, own, cross, *refs):
+    relocate(shifts, pick, own, cross, refs[:-1], refs[-1])
+
+
+def final_kernel(scale, shifts, pick, got, own, cross, *refs):
+    blocks, (relocated, energy, bias) = refs[:-3], refs[-3:]
+    relocate(shifts, pick, own, cross, blocks, relocated)
     devices = got.shape[0]
     low = lax.broadcasted_iota(jnp.int32, pick.shape[1:], 1) < LANES // 2
     parts = jnp.zeros(pick.shape[1:], jnp.float32)
@@ -170,68 +201,74 @@
         return permuted(own, lambda m, c: (m ^ s, c) if c == m % 2 else (m ^ (s - 1), 1 - c))
 
     partner = permuted(greens, lambda m, c: (m, 1 - c))
-    half = permuted(greens, lambda m, c: (m ^ 4, c))
-    cross = permuted(greens, lambda m, c: (m ^ 1, 1 - c))
+    payload = jax.ShapeDtypeStruct((devices, NEAR, LANES), jnp.float32)
+    blank = pl.pallas_call(
+        blank_kernel,
+        out_shape=payload,
+        out_specs=vmem,
+        compiler_params=params,
+        cost_estimate=pl.CostEstimate(flops=4 * 10**9, bytes_accessed=4096, transcendentals=0),
+    )()
+    partner, blank = lax.optimization_barrier((partner, blank))
     own = pl.pallas_call(
         own_kernel,
         out_shape=jax.ShapeDtypeStruct((2, occ, orb), greens.dtype),
         in_specs=[vmem, vmem],
         out_specs=vmem,
         compiler_params=params,
-        cost_estimate=pl.CostEstimate(flops=4 * 10**9, bytes_accessed=4 * occ * orb, transcendentals=0),
+        cost_estimate=pl.CostEstimate(flops=0, bytes_accessed=4 * occ * orb, transcendentals=0),
     )(greens, partner)
     after_own, own = lax.optimization_barrier((cholesky, own))
     other = permuted(after_own, lambda m, c: (m, 1 - c))
-    far = trade(7)
-    beside = [trade(s) for s in [3] + list(range(9, chips, 2))]
-    forwarded = permuted(half, lambda m, c: (m ^ 1, c))
-    held = dict(zip([3] + list(range(9, chips, 2)) + [7], beside + [far]))
-    odds = [3] + list(range(9, chips, 2)) + [5, 7]
+    odds = [7] + list(range(9, chips, 2))
+    trades = [trade(s) for s in odds]
+    near = trade(3)
+    after, own = lax.optimization_barrier((greens, own))
+    cross = permuted(after, lambda m, c: (m ^ 1, 1 - c))
+    last = trade(5)
+    held = dict(zip(odds + [3], trades + [near]))
     shifts = [2**k - 1 for k in range(2, chips.bit_length())]
-    count = 1 + len(beside)
-
-    def cost(blocks):
+    count = 1 + len(trades)
+
+    def compute(kernel, out_shape, blocks, operands, scratch):
         flops = 2 * (2 * blocks * occ) * (2 * chol_dev * occ) * orb
-        return pl.CostEstimate(flops=flops, bytes_accessed=4 * chol_dev * occ * orb, transcendentals=0)
-
-    early = pl.pallas_call(
-        lambda own, cross, *r: early_kernel(own, cross, r[: count - 1], *r[count - 1 :]),
-        out_shape=jax.ShapeDtypeStruct((LANES, 2 * count * occ), jnp.float32),
-        in_specs=[vmem] * (count + 3),
+        return pl.pallas_call(
+            kernel,
+            out_shape=out_shape,
+            in_specs=[vmem] * len(operands),
+            out_specs=vmem,
+            scratch_shapes=[sums_of(blocks, pltpu.VMEM)] if scratch else [],
+            compiler_params=params,
+            cost_estimate=pl.CostEstimate(flops=flops, bytes_accessed=4 * chol_dev * occ * orb, transcendentals=0),
+        )(*operands)
+
+    def sums_of(blocks, kind):
+        return kind((LANES, 2 * blocks * occ), jnp.float32)
+
+    pick = pl.pallas_call(
+        pick_kernel,
+        out_shape=jax.ShapeDtypeStruct((slots, NEAR, LANES), jnp.float32),
+        in_specs=[smem, smem],
         out_specs=vmem,
         compiler_params=params,
-        cost_estimate=cost(count),
-    )(own, cross, *beside, cholesky, other)
-    sent = pl.pallas_call(
-        functools.partial(late_kernel, odds),
-        out_shape=jax.ShapeDtypeStruct((devices, NEAR, LANES), jnp.float32),
-        in_specs=[vmem] * 6,
-        out_specs=vmem,
-        scratch_shapes=[pltpu.VMEM((LANES, 4 * occ), jnp.float32)],
-        compiler_params=params,
-        cost_estimate=cost(2),
-    )(far, half, forwarded, cholesky, other, early)
+        cost_estimate=pl.CostEstimate(flops=4 * 10**9, bytes_accessed=4096, transcendentals=0),
+    )(source, counts)
+    held_own = own
+    own, pick = lax.optimization_barrier((own, pick))
+    early = compute(functools.partial(early_kernel, odds), payload, count, (own, cross, *trades, cholesky, other, blank), True)
+    sent = compute(functools.partial(late_kernel, [3, 5]), payload, 2, (near, last, cholesky, other, early), True)
     got = lax.all_to_all(sent, "walk", split_axis=0, concat_axis=0, tiled=True)
-    relocated, pick = pl.pallas_call(
-        functools.partial(relocate_kernel, shifts),
+    relocated, energy, force_bias = pl.pallas_call(
+        functools.partial(final_kernel, -(0.5 / nchol), shifts),
         out_shape=(
-            jax.ShapeDtypeStruct((slots, occ, orb), jnp.bfloat16),
-            jax.ShapeDtypeStruct((slots, NEAR, LANES), jnp.float32),
-        ),
-        in_specs=[smem, smem] + [vmem] * (2 + len(shifts)),
-        out_specs=[vmem, vmem],
-        compiler_params=params,
-    )(source, counts, own, cross, *[held[s] for s in shifts])
-    energy, force_bias = pl.pallas_call(
-        functools.partial(final_kernel, -(0.5 / nchol)),
-        out_shape=(
+            jax.ShapeDtypeStruct((slots, occ, orb), greens.dtype),
             jax.ShapeDtypeStruct((slots,), jnp.float32),
             jax.ShapeDtypeStruct((slots, nchol), jnp.float32),
         ),
-        in_specs=[vmem, vmem],
-        out_specs=[smem, vmem],
-        compiler_params=params,
-    )(pick, got)
+        in_specs=[vmem] * (4 + len(shifts)),
+        out_specs=[vmem, smem, vmem],
+        compiler_params=params,
+    )(pick, got, own, cross, *[held[s] for s in shifts])
     return relocated, energy, force_bias
 
 

time: 34.2 us -> 30.8 us (0.901)
  blocking collectives: 0 us -> 9.84 us
  starting transfers between devices: 15 us -> 7.44 us
  waiting for transfers between devices: 10.5 us -> 6.73 us
  Pallas kernels: 6.89 us -> 5.83 us
  local copies, waits for them, and re-layouts: 0.82 us -> 0.02 us
    all_to_all x0 -> x1, blocking collectives: none -> 9.84 us  [body(): got = lax.all_to_all(sent, 'walk', split_axis=0, concat_axis=0, tiled=True)]
    all_to_all x1 -> x0, starting transfers between devices: 6.12 us -> none  [body(): got = lax.all_to_all(sent, 'walk', split_axis=0, concat_axis=0, tiled=True)]
    all_to_all x1 -> x0, waiting for transfers between devices: 5.39 us -> none  [body(): got = lax.all_to_all(sent, 'walk', split_axis=0, concat_axis=0, tiled=True)]
    ppermute x7 -> x6, waiting for transfers between devices: 5.11 us -> 6.73 us  [permuted(): lax.ppermute(x, 'walk', [(2 * n + k, 2 * m + c) for m in range(chips) for...]
    ppermute x7 -> x6, starting transfers between devices: 8.9 us -> 7.44 us  [permuted(): lax.ppermute(x, 'walk', [(2 * n + k, 2 * m + c) for m in range(chips) for...]
    pallas_call x4 -> x5, Pallas kernels: 6.89 us -> 5.82 us  [the longest x2 4.52 us: compute(): pl.pallas_call(kernel, out_shape=out_shape, in_specs=[vmem] * len(operand...]
    unnamed x10 -> x8, local copies, waits for them, and re-layouts: 0.82 us -> 0.02 us
  transfers between devices with their start and end apart: 8 -> 6, of which waited for: 5 -> 4; matrix products, arithmetic and copies ran while one was open for 0% -> 0% of each run, Pallas kernels for 10% -> 9%
where the time goes in v3:
time: 30.8 us; the launch traced here: 30.6 us
  blocking collectives  9.84 us (32%)
  starting transfers between devices  7.44 us (24%)
  waiting for transfers between devices  6.73 us (22%)
  Pallas kernels  5.83 us (19%)
  between operations  0.71 us (2%)
    all_to_all x1, blocking collectives, body(): got = lax.all_to_all(sent, 'walk', split_axis=0, concat_axis=0, tiled=True)  9.84 us
    ppermute x6, starting transfers between devices, permuted(): lax.ppermute(x, 'walk', [(2 * n + k, 2 * m + c) for m in range(chips) for...  7.44 us
    ppermute x6, waiting for transfers between devices, permuted(): lax.ppermute(x, 'walk', [(2 * n + k, 2 * m + c) for m in range(chips) for...  6.73 us
    pallas_call x2, Pallas kernels, compute(): pl.pallas_call(kernel, out_shape=out_shape, in_specs=[vmem] * len(operand...  4.52 us
    pallas_call x1, Pallas kernels, body(): pl.pallas_call(functools.partial(final_kernel, -(0.5 / nchol), shifts), o...  0.73 us
  transfers between devices with their start and end apart: 6, of which 4 were waited for; matrix products, arithmetic and copies ran while one was open for 0% of the time, Pallas kernels for 9%

profile of v3, /device:TPU:0, one launch (start us, length us, event | category | flops | bytes accessed | tf_op | source)
XLA Modules:
  0.0 30.6 jit_solution(14970093159795841768)
XLA Ops:
  0.6 0.0 copy-start.1
  0.6 0.0 copy-start
  0.7 0.0 copy-start.3
  0.7 0.0 copy-start.2
  0.7 0.5 %collective-permute-start = (bf16[1,64,384]{2,1,0:T(8,128)(2,1)}, bf16[1,64,384]{2,1,0:T(8,128)(2,1)S(1)}, u32[]{:S(2)}, u32[]{:S(2)}) collective-permute-start(bf16[1,64,384]{2,1,0:T(8,128)(2,1)} %greens.1), channel_id=1, source_target_pairs={{1,0},{0,1},{3,2},{2,3},{5,4},{4,5},{7,6},{6,7},{9,8},{8,9},{11,10... | collective-permute-start | bytes 147464 | tf_op jit(solution)/shard_map/ppermute | solution.py:198
  1.2 1.1 %collective-permute-done.partner = bf16[1,64,384]{2,1,0:T(8,128)(2,1)S(1)} collective-permute-done((bf16[1,64,384]{2,1,0:T(8,128)(2,1)}, bf16[1,64,384]{2,1,0:T(8,128)(2,1)S(1)}, u32[]{:S(2)}, u32[]{:S(2)}) %collective-permute-start) | collective-permute-done | bytes 49184 | tf_op jit(solution)/shard_map/ppermute | solution.py:198
  2.3 0.0 copy-done.1
  2.3 0.0 copy-done
  2.3 0.4 %collective-permute-start.3 = (bf16[32,64,384]{2,1,0:T(8,128)(2,1)S(1)}, bf16[32,64,384]{2,1,0:T(8,128)(2,1)S(1)}, u32[]{:S(2)}, u32[]{:S(2)}) collective-permute-start(bf16[32,64,384]{2,1,0:T(8,128)(2,1)S(1)} %copy-done), channel_id=1, source_target_pairs={{1,0},{0,1},{3,2},{2,3},{5,4},{4,5},{7,6},{6,7},{9,8},{8,9},{11,10... | collective-permute-start | bytes 4718600 | tf_op jit(solution)/shard_map/ppermute | solution.py:198
  2.7 4.7 %collective-permute-start.5 = (bf16[2,64,384]{2,1,0:T(8,128)(2,1)S(1)}, bf16[2,64,384]{2,1,0:T(8,128)(2,1)S(1)}, u32[]{:S(2)}, u32[]{:S(2)}) collective-permute-start(bf16[2,64,384]{2,1,0:T(8,128)(2,1)S(1)} %shard_map.68.own), channel_id=1, source_target_pairs={{14,0},{12,1},{15,2},{13,3},{10,4},{8,5},{11,6},{9,7},{6,8},{4,9},... | collective-permute-start | bytes 294920 | tf_op jit(solution)/shard_map/ppermute | solution.py:198
  7.4 0.2 collective-permute-start.1
  7.7 1.1 %collective-permute-start.4 = (bf16[1,64,384]{2,1,0:T(8,128)(2,1)S(1)}, bf16[1,64,384]{2,1,0:T(8,128)(2,1)S(1)}, u32[]{:S(2)}, u32[]{:S(2)}) collective-permute-start(bf16[1,64,384]{2,1,0:T(8,128)(2,1)S(1)} %copy-done.1), channel_id=1, source_target_pairs={{3,0},{2,1},{1,2},{0,3},{7,4},{6,5},{5,6},{4,7},{11,8},{10,9},{9,1... | collective-permute-start | bytes 147464 | tf_op jit(solution)/shard_map/ppermute | solution.py:198
  8.7 0.5 %collective-permute-start.2 = (bf16[2,64,384]{2,1,0:T(8,128)(2,1)S(1)}, bf16[2,64,384]{2,1,0:T(8,128)(2,1)S(1)}, u32[]{:S(2)}, u32[]{:S(2)}) collective-permute-start(bf16[2,64,384]{2,1,0:T(8,128)(2,1)S(1)} %shard_map.68.own), channel_id=1, source_target_pairs={{10,0},{8,1},{11,2},{9,3},{14,4},{12,5},{15,6},{13,7},{2,8},{0,9},... | collective-permute-start | bytes 294920 | tf_op jit(solution)/shard_map/ppermute | solution.py:198
  9.2 0.0 copy-done.3
  9.2 0.0 copy-done.2
  9.2 0.6 %shard_map.69.pick = f32[2,3,128]{2,1,0:T(4,128)S(1)} custom-call(s32[2]{0:T(128)S(1)} %copy-done.2, s32[16]{0:T(128)S(1)} %copy-done.3), custom_call_target="tpu_custom_call" | custom-call | flops 4000000000 | bytes 4096 | tf_op jit(solution)/shard_map/pallas_call | solution.py:248
  9.8 2.2 %collective-permute-done.4.cross = bf16[1,64,384]{2,1,0:T(8,128)(2,1)S(1)} collective-permute-done((bf16[1,64,384]{2,1,0:T(8,128)(2,1)S(1)}, bf16[1,64,384]{2,1,0:T(8,128)(2,1)S(1)}, u32[]{:S(2)}, u32[]{:S(2)}) %collective-permute-start.4) | collective-permute-done | bytes 49184 | tf_op jit(solution)/shard_map/ppermute | solution.py:198
  12.0 0.1 collective-permute-done.5.refs_0_.refs_1_
  12.1 0.0 collective-permute-done.3.refs_2_.refs_3_
  12.1 2.3 %shard_map.70.refs_4_ = f32[16,3,128]{2,1,0:T(4,128)S(1)} custom-call(bf16[2,64,384]{2,1,0:T(8,128)(2,1)S(1)} %shard_map.68.own, bf16[1,64,384]{2,1,0:T(8,128)(2,1)S(1)} %collective-permute-done.4.cross, bf16[2,64,384]{2,1,0:T(8,128)(2,1)S(1)} %collective-permute-done.5.refs_0_.refs_1_, bf16[32,64,384]{2,1,0:T(8,128)(2,1)S(1)} %copy-done, ...), custom_call_target="tpu_custom_call" | custom-call | flops 805306368 | bytes 3145728 | tf_op jit(solution)/shard_map/pallas_call | solution.py:235
  14.4 3.3 %collective-permute-done.2.refs_1_ = bf16[2,64,384]{2,1,0:T(8,128)(2,1)S(1)} collective-permute-done((bf16[2,64,384]{2,1,0:T(8,128)(2,1)S(1)}, bf16[2,64,384]{2,1,0:T(8,128)(2,1)S(1)}, u32[]{:S(2)}, u32[]{:S(2)}) %collective-permute-start.2) | collective-permute-done | bytes 98336 | tf_op jit(solution)/shard_map/ppermute | solution.py:198
  17.7 0.0 collective-permute-done.1.refs_0_
  17.7 2.3 %shard_map.71 = f32[16,3,128]{2,1,0:T(4,128)S(1)} custom-call(bf16[2,64,384]{2,1,0:T(8,128)(2,1)S(1)} %collective-permute-done.1.refs_0_, bf16[2,64,384]{2,1,0:T(8,128)(2,1)S(1)} %collective-permute-done.2.refs_1_, bf16[32,64,384]{2,1,0:T(8,128)(2,1)S(1)} %copy-done, bf16[32,64,384]{2,1,0:T(8,128)(2,1)S(1)} %collective-permute-done.3.refs_2_.refs_3_, ...), custom_call_target="tpu_custom_call" | custom-call | flops 805306368 | bytes 3145728 | tf_op jit(solution)/shard_map/pallas_call | solution.py:235
  20.0 9.8 %all_to_all.5.got = f32[16,3,128]{2,1,0:T(4,128)S(1)} all-to-all(f32[16,3,128]{2,1,0:T(4,128)S(1)} %shard_map.71), channel_id=1, replica_groups=mesh['rep'=2,'walk'=16] {'walk'}, dimensions={0} | all-to-all | bytes 49152 | tf_op jit(solution)/shard_map/all_to_all | solution.py:260
  29.8 0.7 %shard_map.72 = (bf16[2,64,384]{2,1,0:T(8,128)(2,1)}, f32[2]{0:T(128)}, f32[2,512]{1,0:T(2,128)}) custom-call(f32[2,3,128]{2,1,0:T(4,128)S(1)} %shard_map.69.pick, f32[16,3,128]{2,1,0:T(4,128)S(1)} %all_to_all.5.got, bf16[2,64,384]{2,1,0:T(8,128)(2,1)S(1)} %shard_map.68.own, bf16[1,64,384]{2,1,0:T(8,128)(2,1)S(1)} %collective-permute-done.4.cross, ...), custom_call_target="tpu_custom_call" | custom-call | tf_op jit(solution)/shard_map/pallas_call | solution.py:261
  (2 shorter events, 0.0 us)
Async XLA Ops:
  0.6 1.7 %copy-start.1 = (bf16[1,64,384]{2,1,0:T(8,128)(2,1)S(1)}, bf16[1,64,384]{2,1,0:T(8,128)(2,1)}, u32[]{:S(2)}) copy-start(bf16[1,64,384]{2,1,0:T(8,128)(2,1)} %greens.1) | copy-start | bytes 147460
  0.6 1.7 %copy-start = (bf16[32,64,384]{2,1,0:T(8,128)(2,1)S(1)}, bf16[32,64,384]{2,1,0:T(8,128)(2,1)}, u32[]{:S(2)}) copy-start(bf16[32,64,384]{2,1,0:T(8,128)(2,1)} %refs_2_.1) | copy-start | bytes 4718596
  0.7 8.6 %copy-start.3 = (s32[16]{0:T(128)S(1)}, s32[16]{0:T(128)}, u32[]{:S(2)}) copy-start(s32[16]{0:T(128)} %counts.1) | copy-start | bytes 196
  0.7 8.6 %copy-start.2 = (s32[2]{0:T(128)S(1)}, s32[2]{0:T(128)}, u32[]{:S(2)}) copy-start(s32[2]{0:T(128)} %source.1) | copy-start | bytes 28
  0.7 1.6 %collective-permute-start = (bf16[1,64,384]{2,1,0:T(8,128)(2,1)}, bf16[1,64,384]{2,1,0:T(8,128)(2,1)S(1)}, u32[]{:S(2)}, u32[]{:S(2)}) collective-permute-start(bf16[1,64,384]{2,1,0:T(8,128)(2,1)} %greens.1), channel_id=1, source_target_pairs={{1,0},{0,1},{3,2},{2,3},{5,4},{4,5},{7,6},{6,7},{9,8},{8,9},{11,10... | collective-permute-start | bytes 147464 | tf_op jit(solution)/shard_map/ppermute | solution.py:198
  2.3 9.8 %collective-permute-start.3 = (bf16[32,64,384]{2,1,0:T(8,128)(2,1)S(1)}, bf16[32,64,384]{2,1,0:T(8,128)(2,1)S(1)}, u32[]{:S(2)}, u32[]{:S(2)}) collective-permute-start(bf16[32,64,384]{2,1,0:T(8,128)(2,1)S(1)} %copy-done), channel_id=1, source_target_pairs={{1,0},{0,1},{3,2},{2,3},{5,4},{4,5},{7,6},{6,7},{9,8},{8,9},{11,10... | collective-permute-start | bytes 4718600 | tf_op jit(solution)/shard_map/ppermute | solution.py:198
  2.7 9.4 %collective-permute-start.5 = (bf16[2,64,384]{2,1,0:T(8,128)(2,1)S(1)}, bf16[2,64,384]{2,1,0:T(8,128)(2,1)S(1)}, u32[]{:S(2)}, u32[]{:S(2)}) collective-permute-start(bf16[2,64,384]{2,1,0:T(8,128)(2,1)S(1)} %shard_map.68.own), channel_id=1, source_target_pairs={{14,0},{12,1},{15,2},{13,3},{10,4},{8,5},{11,6},{9,7},{6,8},{4,9},... | collective-permute-start | bytes 294920 | tf_op jit(solution)/shard_map/ppermute | solution.py:198
  7.4 10.3 %collective-permute-start.1 = (bf16[2,64,384]{2,1,0:T(8,128)(2,1)S(1)}, bf16[2,64,384]{2,1,0:T(8,128)(2,1)S(1)}, u32[]{:S(2)}, u32[]{:S(2)}) collective-permute-start(bf16[2,64,384]{2,1,0:T(8,128)(2,1)S(1)} %shard_map.68.own), channel_id=1, source_target_pairs={{6,0},{4,1},{7,2},{5,3},{2,4},{0,5},{3,6},{1,7},{14,8},{12,9},{15,... | collective-permute-start | bytes 294920 | tf_op jit(solution)/shard_map/ppermute | solution.py:198
  7.7 4.4 %collective-permute-start.4 = (bf16[1,64,384]{2,1,0:T(8,128)(2,1)S(1)}, bf16[1,64,384]{2,1,0:T(8,128)(2,1)S(1)}, u32[]{:S(2)}, u32[]{:S(2)}) collective-permute-start(bf16[1,64,384]{2,1,0:T(8,128)(2,1)S(1)} %copy-done.1), channel_id=1, source_target_pairs={{3,0},{2,1},{1,2},{0,3},{7,4},{6,5},{5,6},{4,7},{11,8},{10,9},{9,1... | collective-permute-start | bytes 147464 | tf_op jit(solution)/shard_map/ppermute | solution.py:198
  8.7 9.0 %collective-permute-start.2 = (bf16[2,64,384]{2,1,0:T(8,128)(2,1)S(1)}, bf16[2,64,384]{2,1,0:T(8,128)(2,1)S(1)}, u32[]{:S(2)}, u32[]{:S(2)}) collective-permute-start(bf16[2,64,384]{2,1,0:T(8,128)(2,1)S(1)} %shard_map.68.own), channel_id=1, source_target_pairs={{10,0},{8,1},{11,2},{9,3},{14,4},{12,5},{15,6},{13,7},{2,8},{0,9},... | collective-permute-start | bytes 294920 | tf_op jit(solution)/shard_map/ppermute | solution.py:198

commit v4 on v3

--- a/solution.py
+++ b/solution.py
@@ -11,6 +11,7 @@
 LANES = 128
 SUB = 8
 NEAR = 3
+SINGLES = {"own": 0, "cross": 3, "half": 8, "forwarded": 10}
 STEP = 8
 
 
@@ -88,16 +89,30 @@
     own[1] = partner[0]
 
 
-def walker_ids(odds):
+def walker_ids(tiles):
     me = lax.axis_index("walk")
     chip, core = me // 2, me % 2
     plain = core == chip % 2
     ids = []
-    for s in odds:
-        there = chip ^ jnp.where(plain, s, s - 1)
-        lead = jnp.where(plain, core, 1 - core)
-        ids += [2 * there + lead, 2 * there + 1 - lead]
+    for tile in tiles:
+        if isinstance(tile, tuple):
+            ids += [me ^ SINGLES[name] for name in tile]
+        else:
+            there = chip ^ jnp.where(plain, tile, tile - 1)
+            lead = jnp.where(plain, core, 1 - core)
+            ids += [2 * there + lead, 2 * there + 1 - lead]
     return ids
+
+
+def values_of(tiles, refs):
+    refs = list(refs)
+    values = []
+    for tile in tiles:
+        if isinstance(tile, tuple):
+            values.append(jnp.stack([refs.pop(0)[0] for _ in tile]))
+        else:
+            values.append(refs.pop(0)[...])
+    return values
 
 
 def send(sent, rows, ids):
@@ -107,41 +122,34 @@
             sent[lax.rem(walker + 1 - near + devices, devices), near : near + 1, :] = rows[r : r + 1]
 
 
-def early_kernel(odds, own, cross, *refs):
-    blocks, (mine, other, blank, sent, sums) = refs[:-5], refs[-5:]
-    me = lax.axis_index("walk")
-    chip, core = me // 2, me % 2
-    values = [jnp.concatenate([own[0:1], cross[...]], axis=0)] + [b[...] for b in blocks]
-    block_sums(values, mine, other, sums, chip % 2, core)
-    sent[...] = blank[...]
-    rows = walker_rows(sums[...], own.shape[1])
-    send(sent, rows, [me, 2 * (chip ^ 1) + 1 - core] + walker_ids(odds))
-
-
-def next_kernel(block, mine, other, sums):
-    me = lax.axis_index("walk")
-    block_sums([block[...]], mine, other, sums, (me // 2) % 2, me % 2)
-
-
-def late_kernel(odds, *refs):
-    blocks, (mine, other, early, sent, sums) = refs[:-5], refs[-5:]
-    me = lax.axis_index("walk")
-    block_sums([b[...] for b in blocks], mine, other, sums, (me // 2) % 2, me % 2)
-    sent[...] = early[...]
-    send(sent, walker_rows(sums[...], blocks[0].shape[1]), walker_ids(odds))
+def compute_kernel(tiles, *refs):
+    blocks, (mine, other, before, sent, sums) = refs[:-5], refs[-5:]
+    me = lax.axis_index("walk")
+    block_sums(values_of(tiles, blocks), mine, other, sums, (me // 2) % 2, me % 2)
+    sent[...] = before[...]
+    send(sent, walker_rows(sums[...], blocks[0].shape[1]), walker_ids(tiles))
+
+
+def copy_kernel(x, y):
+    y[...] = x[...]
 
 
 def blank_kernel(sent):
     sent[...] = jnp.zeros_like(sent)
 
 
-def pick_kernel(source, counts, pick):
-    me = lax.axis_index("walk")
-    devices = counts.shape[0]
-    row = lax.broadcasted_iota(jnp.int32, pick.shape[1:], 0)
-    for t in range(pick.shape[0]):
-        near = lax.rem(source[t] - me + 1 + devices, devices)
-        pick[t] = jnp.where((row == near) & (t < counts[me]), 1.0, 0.0)
+def picks(source, counts, slots):
+    me = lax.axis_index("walk")
+    devices = counts.shape[1]
+    count = jnp.sum(jnp.where(lax.broadcasted_iota(jnp.int32, counts.shape, 1) == me, counts[...], 0), axis=1, keepdims=True)
+    row = lax.broadcasted_iota(jnp.int32, (NEAR, LANES), 0)
+    found = []
+    for t in range(slots):
+        walker = jnp.where(lax.broadcasted_iota(jnp.int32, source.shape, 1) == t, source[...], 0)
+        near = jnp.sum(walker, axis=1, keepdims=True) - me + 1
+        near = jnp.where(near < 0, near + devices, jnp.where(near >= devices, near - devices, near))
+        found.append(jnp.where((row == near) & (count > t), 1.0, 0.0))
+    return found
 
 
 def relocate(shifts, pick, own, cross, blocks, relocated):
@@ -156,7 +164,7 @@
     for t in range(relocated.shape[0]):
         value = jnp.zeros(relocated.shape[1:], jnp.float32)
         for near, walker in enumerate((before, own[0], after)):
-            weight = jnp.concatenate([pick[t, near : near + 1]] * (relocated.shape[2] // LANES), axis=1)
+            weight = jnp.concatenate([pick[t][near : near + 1]] * (relocated.shape[2] // LANES), axis=1)
             value = jnp.where(weight > 0, walker.astype(jnp.float32), value)
         relocated[t] = value.astype(relocated.dtype)
 
@@ -165,12 +173,13 @@
     relocate(shifts, pick, own, cross, refs[:-1], refs[-1])
 
 
-def final_kernel(scale, shifts, pick, got, own, cross, *refs):
+def final_kernel(scale, shifts, source, counts, got, own, cross, *refs):
+    pick = picks(source, counts, refs[-1].shape[0])
     blocks, (relocated, energy, bias) = refs[:-3], refs[-3:]
     relocate(shifts, pick, own, cross, blocks, relocated)
     devices = got.shape[0]
-    low = lax.broadcasted_iota(jnp.int32, pick.shape[1:], 1) < LANES // 2
-    parts = jnp.zeros(pick.shape[1:], jnp.float32)
+    low = lax.broadcasted_iota(jnp.int32, pick[0].shape, 1) < LANES // 2
+    parts = jnp.zeros(pick[0].shape, jnp.float32)
     for q in range(devices // 4):
         even = got[4 * q] + got[4 * q + 1]
         odd = got[4 * q + 2] + got[4 * q + 3]
@@ -202,6 +211,7 @@
 
     partner = permuted(greens, lambda m, c: (m, 1 - c))
     payload = jax.ShapeDtypeStruct((devices, NEAR, LANES), jnp.float32)
+    half = permuted(greens, lambda m, c: (m ^ 4, c))
     blank = pl.pallas_call(
         blank_kernel,
         out_shape=payload,
@@ -220,43 +230,41 @@
     )(greens, partner)
     after_own, own = lax.optimization_barrier((cholesky, own))
     other = permuted(after_own, lambda m, c: (m, 1 - c))
-    odds = [7] + list(range(9, chips, 2))
-    trades = [trade(s) for s in odds]
+    far = trade(7)
     near = trade(3)
-    after, own = lax.optimization_barrier((greens, own))
-    cross = permuted(after, lambda m, c: (m ^ 1, 1 - c))
-    last = trade(5)
-    held = dict(zip(odds + [3], trades + [near]))
+    more = list(range(9, chips, 2))
+    held = {7: far, 3: near, **{s: trade(s) for s in more}}
+    forwarded = permuted(half, lambda m, c: (m ^ 1, c))
+    cross = permuted(greens, lambda m, c: (m ^ 1, 1 - c))
     shifts = [2**k - 1 for k in range(2, chips.bit_length())]
-    count = 1 + len(trades)
-
-    def compute(kernel, out_shape, blocks, operands, scratch):
-        flops = 2 * (2 * blocks * occ) * (2 * chol_dev * occ) * orb
+    blank = pl.pallas_call(
+        copy_kernel,
+        out_shape=payload,
+        in_specs=[vmem],
+        out_specs=vmem,
+        compiler_params=params,
+        cost_estimate=pl.CostEstimate(flops=4 * 10**9, bytes_accessed=4096, transcendentals=0),
+    )(blank)
+    singles = {"own": own, "cross": cross, "half": half, "forwarded": forwarded}
+
+    def compute(tiles, before):
+        flops = 2 * (2 * len(tiles) * occ) * (2 * chol_dev * occ) * orb
+        operands = []
+        for tile in tiles:
+            operands += [singles[name] for name in tile] if isinstance(tile, tuple) else [held[tile]]
+        operands += [cholesky, other, before]
         return pl.pallas_call(
-            kernel,
-            out_shape=out_shape,
+            functools.partial(compute_kernel, tiles),
+            out_shape=payload,
             in_specs=[vmem] * len(operands),
             out_specs=vmem,
-            scratch_shapes=[sums_of(blocks, pltpu.VMEM)] if scratch else [],
+            scratch_shapes=[pltpu.VMEM((LANES, 2 * len(tiles) * occ), jnp.float32)],
             compiler_params=params,
             cost_estimate=pl.CostEstimate(flops=flops, bytes_accessed=4 * chol_dev * occ * orb, transcendentals=0),
         )(*operands)
 
-    def sums_of(blocks, kind):
-        return kind((LANES, 2 * blocks * occ), jnp.float32)
-
-    pick = pl.pallas_call(
-        pick_kernel,
-        out_shape=jax.ShapeDtypeStruct((slots, NEAR, LANES), jnp.float32),
-        in_specs=[smem, smem],
-        out_specs=vmem,
-        compiler_params=params,
-        cost_estimate=pl.CostEstimate(flops=4 * 10**9, bytes_accessed=4096, transcendentals=0),
-    )(source, counts)
-    held_own = own
-    own, pick = lax.optimization_barrier((own, pick))
-    early = compute(functools.partial(early_kernel, odds), payload, count, (own, cross, *trades, cholesky, other, blank), True)
-    sent = compute(functools.partial(late_kernel, [3, 5]), payload, 2, (near, last, cholesky, other, early), True)
+    sent = compute([("own","half"),3] + more, blank)
+    sent = compute([7,("cross","forwarded")], sent)
     got = lax.all_to_all(sent, "walk", split_axis=0, concat_axis=0, tiled=True)
     relocated, energy, force_bias = pl.pallas_call(
         functools.partial(final_kernel, -(0.5 / nchol), shifts),
@@ -265,10 +273,10 @@
             jax.ShapeDtypeStruct((slots,), jnp.float32),
             jax.ShapeDtypeStruct((slots, nchol), jnp.float32),
         ),
-        in_specs=[vmem] * (4 + len(shifts)),
+        in_specs=[vmem] * (5 + len(shifts)),
         out_specs=[vmem, smem, vmem],
         compiler_params=params,
-    )(pick, got, own, cross, *[held[s] for s in shifts])
+    )(source.reshape(1, -1), counts.reshape(1, -1), got, own, cross, *[held[s] for s in shifts])
     return relocated, energy, force_bias
 
 

time: 30.8 us -> 29.8 us (0.968)
  waiting for transfers between devices: 6.73 us -> 4.85 us
  starting transfers between devices: 7.44 us -> 9.23 us
  Pallas kernels: 5.83 us -> 5.33 us
  blocking collectives: 9.84 us -> 9.46 us
    ppermute x6 -> x7, waiting for transfers between devices: 6.73 us -> 4.85 us  [permuted(): lax.ppermute(x, 'walk', [(2 * n + k, 2 * m + c) for m in range(chips) for...]
    ppermute x6 -> x7, starting transfers between devices: 7.44 us -> 9.23 us  [permuted(): lax.ppermute(x, 'walk', [(2 * n + k, 2 * m + c) for m in range(chips) for...]
    pallas_call x3, Pallas kernels: 5.08 us -> 4.52 us  [the longest x2 4.52 us: compute(): pl.pallas_call(functools.partial(compute_kernel, tiles), out_shape=payloa...]
    all_to_all x1, blocking collectives: 9.84 us -> 9.46 us  [body(): got = lax.all_to_all(sent, 'walk', split_axis=0, concat_axis=0, tiled=True)]
  transfers between devices with their start and end apart: 6 -> 7, of which waited for: 4 -> 3; matrix products, arithmetic and copies ran while one was open for 0% -> 0% of each run, Pallas kernels for 9% -> 8%
where the time goes in v4:
time: 29.8 us; the launch traced here: 29.6 us
  blocking collectives  9.46 us (32%)
  starting transfers between devices  9.23 us (31%)
  Pallas kernels  5.33 us (18%)
  waiting for transfers between devices  4.85 us (16%)
  between operations  0.73 us (2%)
    all_to_all x1, blocking collectives, body(): got = lax.all_to_all(sent, 'walk', split_axis=0, concat_axis=0, tiled=True)  9.46 us
    ppermute x7, starting transfers between devices, permuted(): lax.ppermute(x, 'walk', [(2 * n + k, 2 * m + c) for m in range(chips) for...  9.23 us
    ppermute x7, waiting for transfers between devices, permuted(): lax.ppermute(x, 'walk', [(2 * n + k, 2 * m + c) for m in range(chips) for...  4.85 us
    pallas_call x2, Pallas kernels, compute(): pl.pallas_call(functools.partial(compute_kernel, tiles), out_shape=payloa...  4.52 us
    pallas_call x1, Pallas kernels, body(): pl.pallas_call(functools.partial(final_kernel, -(0.5 / nchol), shifts), o...  0.79 us
  transfers between devices with their start and end apart: 7, of which 3 were waited for; matrix products, arithmetic and copies ran while one was open for 0% of the time, Pallas kernels for 8%

profile of v4, /device:TPU:0, one launch (start us, length us, event | category | flops | bytes accessed | tf_op | source)
XLA Modules:
  0.0 29.6 jit_solution(11172689765106345808)
XLA Ops:
  0.6 0.0 copy-start.1
  0.6 0.0 copy-start
  0.6 0.5 %collective-permute-start = (bf16[1,64,384]{2,1,0:T(8,128)(2,1)}, bf16[1,64,384]{2,1,0:T(8,128)(2,1)S(1)}, u32[]{:S(2)}, u32[]{:S(2)}) collective-permute-start(bf16[1,64,384]{2,1,0:T(8,128)(2,1)} %greens.1), channel_id=1, source_target_pairs={{1,0},{0,1},{3,2},{2,3},{5,4},{4,5},{7,6},{6,7},{9,8},{8,9},{11,10... | collective-permute-start | bytes 147464 | tf_op jit(solution)/shard_map/ppermute | solution.py:207
  1.2 1.1 %collective-permute-done.partner = bf16[1,64,384]{2,1,0:T(8,128)(2,1)S(1)} collective-permute-done((bf16[1,64,384]{2,1,0:T(8,128)(2,1)}, bf16[1,64,384]{2,1,0:T(8,128)(2,1)S(1)}, u32[]{:S(2)}, u32[]{:S(2)}) %collective-permute-start) | collective-permute-done | bytes 49184 | tf_op jit(solution)/shard_map/ppermute | solution.py:207
  2.3 0.0 copy-done.1
  2.3 0.0 copy-done
  2.3 0.4 %collective-permute-start.5 = (bf16[32,64,384]{2,1,0:T(8,128)(2,1)S(1)}, bf16[32,64,384]{2,1,0:T(8,128)(2,1)S(1)}, u32[]{:S(2)}, u32[]{:S(2)}) collective-permute-start(bf16[32,64,384]{2,1,0:T(8,128)(2,1)S(1)} %copy-done), channel_id=1, source_target_pairs={{1,0},{0,1},{3,2},{2,3},{5,4},{4,5},{7,6},{6,7},{9,8},{8,9},{11,10... | collective-permute-start | bytes 4718600 | tf_op jit(solution)/shard_map/ppermute | solution.py:207
  2.7 3.7 %collective-permute-start.3 = (bf16[1,64,384]{2,1,0:T(8,128)(2,1)S(1)}, bf16[1,64,384]{2,1,0:T(8,128)(2,1)S(1)}, u32[]{:S(2)}, u32[]{:S(2)}) collective-permute-start(bf16[1,64,384]{2,1,0:T(8,128)(2,1)S(1)} %copy-done.1), channel_id=1, source_target_pairs={{8,0},{9,1},{10,2},{11,3},{12,4},{13,5},{14,6},{15,7},{0,8},{1,9},... | collective-permute-start | bytes 147464 | tf_op jit(solution)/shard_map/ppermute | solution.py:207
  6.4 1.2 %collective-permute-start.2 = (bf16[1,64,384]{2,1,0:T(8,128)(2,1)S(1)}, bf16[1,64,384]{2,1,0:T(8,128)(2,1)S(1)}, u32[]{:S(2)}, u32[]{:S(2)}) collective-permute-start(bf16[1,64,384]{2,1,0:T(8,128)(2,1)S(1)} %copy-done.1), channel_id=1, source_target_pairs={{3,0},{2,1},{1,2},{0,3},{7,4},{6,5},{5,6},{4,7},{11,8},{10,9},{9,1... | collective-permute-start | bytes 147464 | tf_op jit(solution)/shard_map/ppermute | solution.py:207
  7.6 1.6 %collective-permute-start.6 = (bf16[2,64,384]{2,1,0:T(8,128)(2,1)S(1)}, bf16[2,64,384]{2,1,0:T(8,128)(2,1)S(1)}, u32[]{:S(2)}, u32[]{:S(2)}) collective-permute-start(bf16[2,64,384]{2,1,0:T(8,128)(2,1)S(1)} %shard_map.68.refs_0_.own), channel_id=1, source_target_pairs={{6,0},{4,1},{7,2},{5,3},{2,4},{0,5},{3,6},{1,7},{14,8},{12,9},{15,... | collective-permute-start | bytes 294920 | tf_op jit(solution)/shard_map/ppermute | solution.py:207
  9.3 0.0 collective-permute-start.1
  9.3 0.0 collective-permute-done.3.refs_1_
  9.3 1.7 %collective-permute-start.4 = (bf16[1,64,384]{2,1,0:T(8,128)(2,1)S(1)}, bf16[1,64,384]{2,1,0:T(8,128)(2,1)S(1)}, u32[]{:S(2)}, u32[]{:S(2)}) collective-permute-start(bf16[1,64,384]{2,1,0:T(8,128)(2,1)S(1)} %collective-permute-done.3.refs_1_), channel_id=1, source_target_pairs={{2,0},{3,1},{0,2},{1,3},{6,4},{7,5},{4,6},{5,7},{10,8},{11,9},{8,1... | collective-permute-start | bytes 147464 | tf_op jit(solution)/shard_map/ppermute | solution.py:207
  11.0 2.2 %collective-permute-done.6.refs_2_.refs_0_ = bf16[2,64,384]{2,1,0:T(8,128)(2,1)S(1)} collective-permute-done((bf16[2,64,384]{2,1,0:T(8,128)(2,1)S(1)}, bf16[2,64,384]{2,1,0:T(8,128)(2,1)S(1)}, u32[]{:S(2)}, u32[]{:S(2)}) %collective-permute-start.6) | collective-permute-done | bytes 98336 | tf_op jit(solution)/shard_map/ppermute | solution.py:207
  13.3 0.0 collective-permute-done.5.refs_4_
  13.3 2.3 %shard_map.70.refs_5_ = f32[16,3,128]{2,1,0:T(4,128)S(1)} custom-call(bf16[2,64,384]{2,1,0:T(8,128)(2,1)S(1)} %shard_map.68.refs_0_.own, bf16[1,64,384]{2,1,0:T(8,128)(2,1)S(1)} %collective-permute-done.3.refs_1_, bf16[2,64,384]{2,1,0:T(8,128)(2,1)S(1)} %collective-permute-done.6.refs_2_.refs_0_, bf16[32,64,384]{2,1,0:T(8,128)(2,1)S(1)} %copy-done, ...), custom_call_target="tpu_custom_call" | custom-call | flops 805306368 | bytes 3145728 | tf_op jit(solution)/shard_map/pallas_call | solution.py:256
  15.5 0.0 copy-start.2
  15.6 0.0 copy-start.3
  15.6 0.0 collective-permute-done.2.refs_1_.cross
  15.6 0.0 collective-permute-done.4.refs_2_
  15.6 1.5 %collective-permute-done.1.refs_0_.refs_1_ = bf16[2,64,384]{2,1,0:T(8,128)(2,1)S(1)} collective-permute-done((bf16[2,64,384]{2,1,0:T(8,128)(2,1)S(1)}, bf16[2,64,384]{2,1,0:T(8,128)(2,1)S(1)}, u32[]{:S(2)}, u32[]{:S(2)}) %collective-permute-start.1) | collective-permute-done | bytes 98336 | tf_op jit(solution)/shard_map/ppermute | solution.py:207
  17.1 2.3 %shard_map.71 = f32[16,3,128]{2,1,0:T(4,128)S(1)} custom-call(bf16[2,64,384]{2,1,0:T(8,128)(2,1)S(1)} %collective-permute-done.1.refs_0_.refs_1_, bf16[1,64,384]{2,1,0:T(8,128)(2,1)S(1)} %collective-permute-done.2.refs_1_.cross, bf16[1,64,384]{2,1,0:T(8,128)(2,1)S(1)} %collective-permute-done.4.refs_2_, bf16[32,64,384]{2,1,0:T(8,128)(2,1)S(1)} %copy-done, ...), custom_call_target="tpu_custom_call" | custom-call | flops 805306368 | bytes 3145728 | tf_op jit(solution)/shard_map/pallas_call | solution.py:256
  19.4 9.5 %all_to_all.5.got = f32[16,3,128]{2,1,0:T(4,128)S(1)} all-to-all(f32[16,3,128]{2,1,0:T(4,128)S(1)} %shard_map.71), channel_id=1, replica_groups=mesh['rep'=2,'walk'=16] {'walk'}, dimensions={0} | all-to-all | bytes 49152 | tf_op jit(solution)/shard_map/all_to_all | solution.py:268
  28.8 0.0 copy-done.2
  28.9 0.0 copy-done.3
  28.9 0.8 %shard_map.72 = (bf16[2,64,384]{2,1,0:T(8,128)(2,1)}, f32[2]{0:T(128)}, f32[2,512]{1,0:T(2,128)}) custom-call(s32[1,2]{1,0:T(1,128)S(1)} %bitcast.2, s32[1,16]{1,0:T(1,128)S(1)} %bitcast.3, f32[16,3,128]{2,1,0:T(4,128)S(1)} %all_to_all.5.got, bf16[2,64,384]{2,1,0:T(8,128)(2,1)S(1)} %shard_map.68.refs_0_.own, ...), custom_call_target="tpu_custom_call" | custom-call | tf_op jit(solution)/shard_map/pallas_call | solution.py:269
  (3 shorter events, 0.0 us)
Async XLA Ops:
  0.6 1.6 %copy-start.1 = (bf16[1,64,384]{2,1,0:T(8,128)(2,1)S(1)}, bf16[1,64,384]{2,1,0:T(8,128)(2,1)}, u32[]{:S(2)}) copy-start(bf16[1,64,384]{2,1,0:T(8,128)(2,1)} %greens.1) | copy-start | bytes 147460
  0.6 1.6 %copy-start = (bf16[32,64,384]{2,1,0:T(8,128)(2,1)S(1)}, bf16[32,64,384]{2,1,0:T(8,128)(2,1)}, u32[]{:S(2)}) copy-start(bf16[32,64,384]{2,1,0:T(8,128)(2,1)} %refs_3_.3) | copy-start | bytes 4718596
  0.6 1.6 %collective-permute-start = (bf16[1,64,384]{2,1,0:T(8,128)(2,1)}, bf16[1,64,384]{2,1,0:T(8,128)(2,1)S(1)}, u32[]{:S(2)}, u32[]{:S(2)}) collective-permute-start(bf16[1,64,384]{2,1,0:T(8,128)(2,1)} %greens.1), channel_id=1, source_target_pairs={{1,0},{0,1},{3,2},{2,3},{5,4},{4,5},{7,6},{6,7},{9,8},{8,9},{11,10... | collective-permute-start | bytes 147464 | tf_op jit(solution)/shard_map/ppermute | solution.py:207
  2.3 11.0 %collective-permute-start.5 = (bf16[32,64,384]{2,1,0:T(8,128)(2,1)S(1)}, bf16[32,64,384]{2,1,0:T(8,128)(2,1)S(1)}, u32[]{:S(2)}, u32[]{:S(2)}) collective-permute-start(bf16[32,64,384]{2,1,0:T(8,128)(2,1)S(1)} %copy-done), channel_id=1, source_target_pairs={{1,0},{0,1},{3,2},{2,3},{5,4},{4,5},{7,6},{6,7},{9,8},{8,9},{11,10... | collective-permute-start | bytes 4718600 | tf_op jit(solution)/shard_map/ppermute | solution.py:207
  2.7 6.6 %collective-permute-start.3 = (bf16[1,64,384]{2,1,0:T(8,128)(2,1)S(1)}, bf16[1,64,384]{2,1,0:T(8,128)(2,1)S(1)}, u32[]{:S(2)}, u32[]{:S(2)}) collective-permute-start(bf16[1,64,384]{2,1,0:T(8,128)(2,1)S(1)} %copy-done.1), channel_id=1, source_target_pairs={{8,0},{9,1},{10,2},{11,3},{12,4},{13,5},{14,6},{15,7},{0,8},{1,9},... | collective-permute-start | bytes 147464 | tf_op jit(solution)/shard_map/ppermute | solution.py:207
  6.4 9.1 %collective-permute-start.2 = (bf16[1,64,384]{2,1,0:T(8,128)(2,1)S(1)}, bf16[1,64,384]{2,1,0:T(8,128)(2,1)S(1)}, u32[]{:S(2)}, u32[]{:S(2)}) collective-permute-start(bf16[1,64,384]{2,1,0:T(8,128)(2,1)S(1)} %copy-done.1), channel_id=1, source_target_pairs={{3,0},{2,1},{1,2},{0,3},{7,4},{6,5},{5,6},{4,7},{11,8},{10,9},{9,1... | collective-permute-start | bytes 147464 | tf_op jit(solution)/shard_map/ppermute | solution.py:207
  7.6 5.6 %collective-permute-start.6 = (bf16[2,64,384]{2,1,0:T(8,128)(2,1)S(1)}, bf16[2,64,384]{2,1,0:T(8,128)(2,1)S(1)}, u32[]{:S(2)}, u32[]{:S(2)}) collective-permute-start(bf16[2,64,384]{2,1,0:T(8,128)(2,1)S(1)} %shard_map.68.refs_0_.own), channel_id=1, source_target_pairs={{6,0},{4,1},{7,2},{5,3},{2,4},{0,5},{3,6},{1,7},{14,8},{12,9},{15,... | collective-permute-start | bytes 294920 | tf_op jit(solution)/shard_map/ppermute | solution.py:207
  9.3 7.8 %collective-permute-start.1 = (bf16[2,64,384]{2,1,0:T(8,128)(2,1)S(1)}, bf16[2,64,384]{2,1,0:T(8,128)(2,1)S(1)}, u32[]{:S(2)}, u32[]{:S(2)}) collective-permute-start(bf16[2,64,384]{2,1,0:T(8,128)(2,1)S(1)} %shard_map.68.refs_0_.own), channel_id=1, source_target_pairs={{14,0},{12,1},{15,2},{13,3},{10,4},{8,5},{11,6},{9,7},{6,8},{4,9},... | collective-permute-start | bytes 294920 | tf_op jit(solution)/shard_map/ppermute | solution.py:207
  9.3 6.3 %collective-permute-start.4 = (bf16[1,64,384]{2,1,0:T(8,128)(2,1)S(1)}, bf16[1,64,384]{2,1,0:T(8,128)(2,1)S(1)}, u32[]{:S(2)}, u32[]{:S(2)}) collective-permute-start(bf16[1,64,384]{2,1,0:T(8,128)(2,1)S(1)} %collective-permute-done.3.refs_1_), channel_id=1, source_target_pairs={{2,0},{3,1},{0,2},{1,3},{6,4},{7,5},{4,6},{5,7},{10,8},{11,9},{8,1... | collective-permute-start | bytes 147464 | tf_op jit(solution)/shard_map/ppermute | solution.py:207
  15.5 13.3 %copy-start.2 = (s32[2]{0:T(128)S(1)}, s32[2]{0:T(128)}, u32[]{:S(2)}) copy-start(s32[2]{0:T(128)} %param.5) | copy-start | bytes 28
  15.6 13.3 %copy-start.3 = (s32[16]{0:T(128)S(1)}, s32[16]{0:T(128)}, u32[]{:S(2)}) copy-start(s32[16]{0:T(128)} %param.6) | copy-start | bytes 196

commit v5 on v4

--- a/solution.py
+++ b/solution.py
@@ -119,7 +119,8 @@
     devices = sent.shape[0]
     for r, walker in enumerate(ids):
         for near in range(NEAR):
-            sent[lax.rem(walker + 1 - near + devices, devices), near : near + 1, :] = rows[r : r + 1]
+            to = lax.rem(walker + 1 - near + devices, devices)
+            sent[to, :, near * LANES : (near + 1) * LANES] = rows[r : r + 1]
 
 
 def compute_kernel(tiles, *refs):
@@ -169,10 +170,6 @@
         relocated[t] = value.astype(relocated.dtype)
 
 
-def relocate_kernel(shifts, pick, own, cross, *refs):
-    relocate(shifts, pick, own, cross, refs[:-1], refs[-1])
-
-
 def final_kernel(scale, shifts, source, counts, got, own, cross, *refs):
     pick = picks(source, counts, refs[-1].shape[0])
     blocks, (relocated, energy, bias) = refs[:-3], refs[-3:]
@@ -183,6 +180,7 @@
     for q in range(devices // 4):
         even = got[4 * q] + got[4 * q + 1]
         odd = got[4 * q + 2] + got[4 * q + 3]
+        even, odd = (jnp.concatenate([x[:, r * LANES : (r + 1) * LANES] for r in range(NEAR)], axis=0) for x in (even, odd))
         tile = jnp.where(low, even, odd)
         parts += jnp.where(low, odd, even)
         for t in range(bias.shape[0]):
@@ -210,7 +208,7 @@
         return permuted(own, lambda m, c: (m ^ s, c) if c == m % 2 else (m ^ (s - 1), 1 - c))
 
     partner = permuted(greens, lambda m, c: (m, 1 - c))
-    payload = jax.ShapeDtypeStruct((devices, NEAR, LANES), jnp.float32)
+    payload = jax.ShapeDtypeStruct((devices, 1, NEAR * LANES), jnp.float32)
     half = permuted(greens, lambda m, c: (m ^ 4, c))
     blank = pl.pallas_call(
         blank_kernel,
@@ -263,8 +261,8 @@
             cost_estimate=pl.CostEstimate(flops=flops, bytes_accessed=4 * chol_dev * occ * orb, transcendentals=0),
         )(*operands)
 
-    sent = compute([("own","half"),3] + more, blank)
-    sent = compute([7,("cross","forwarded")], sent)
+    sent = compute([("own", "half"), 3] + more, blank)
+    sent = compute([7, ("cross", "forwarded")], sent)
     got = lax.all_to_all(sent, "walk", split_axis=0, concat_axis=0, tiled=True)
     relocated, energy, force_bias = pl.pallas_call(
         functools.partial(final_kernel, -(0.5 / nchol), shifts),

time: 29.8 us -> 29.8 us (level)
  no operation moved by 1% of the time
where the time goes in v5:
time: 29.8 us; the launch traced here: 29.6 us
  blocking collectives  9.39 us (32%)
  starting transfers between devices  9.23 us (31%)
  Pallas kernels  5.32 us (18%)
  waiting for transfers between devices  4.85 us (16%)
  between operations  0.76 us (3%)
    all_to_all x1, blocking collectives, body(): got = lax.all_to_all(sent, 'walk', split_axis=0, concat_axis=0, tiled=True)  9.39 us
    ppermute x7, starting transfers between devices, permuted(): lax.ppermute(x, 'walk', [(2 * n + k, 2 * m + c) for m in range(chips) for...  9.23 us
    ppermute x7, waiting for transfers between devices, permuted(): lax.ppermute(x, 'walk', [(2 * n + k, 2 * m + c) for m in range(chips) for...  4.85 us
    pallas_call x2, Pallas kernels, compute(): pl.pallas_call(functools.partial(compute_kernel, tiles), out_shape=payloa...  4.51 us
    pallas_call x1, Pallas kernels, body(): pl.pallas_call(functools.partial(final_kernel, -(0.5 / nchol), shifts), o...  0.79 us
  transfers between devices with their start and end apart: 7, of which 3 were waited for; matrix products, arithmetic and copies ran while one was open for 0% of the time, Pallas kernels for 8%

profile of v5, /device:TPU:0, one launch (start us, length us, event | category | flops | bytes accessed | tf_op | source)
XLA Modules:
  0.0 29.6 jit_solution(16879617276436427421)
XLA Ops:
  0.6 0.0 copy-start.1
  0.6 0.0 copy-start
  0.6 0.5 %collective-permute-start = (bf16[1,64,384]{2,1,0:T(8,128)(2,1)}, bf16[1,64,384]{2,1,0:T(8,128)(2,1)S(1)}, u32[]{:S(2)}, u32[]{:S(2)}) collective-permute-start(bf16[1,64,384]{2,1,0:T(8,128)(2,1)} %greens.1), channel_id=1, source_target_pairs={{1,0},{0,1},{3,2},{2,3},{5,4},{4,5},{7,6},{6,7},{9,8},{8,9},{11,10... | collective-permute-start | bytes 147464 | tf_op jit(solution)/shard_map/ppermute | solution.py:205
  1.2 1.1 %collective-permute-done.partner = bf16[1,64,384]{2,1,0:T(8,128)(2,1)S(1)} collective-permute-done((bf16[1,64,384]{2,1,0:T(8,128)(2,1)}, bf16[1,64,384]{2,1,0:T(8,128)(2,1)S(1)}, u32[]{:S(2)}, u32[]{:S(2)}) %collective-permute-start) | collective-permute-done | bytes 49184 | tf_op jit(solution)/shard_map/ppermute | solution.py:205
  2.3 0.0 copy-done.1
  2.3 0.0 copy-done
  2.3 0.4 %collective-permute-start.5 = (bf16[32,64,384]{2,1,0:T(8,128)(2,1)S(1)}, bf16[32,64,384]{2,1,0:T(8,128)(2,1)S(1)}, u32[]{:S(2)}, u32[]{:S(2)}) collective-permute-start(bf16[32,64,384]{2,1,0:T(8,128)(2,1)S(1)} %copy-done), channel_id=1, source_target_pairs={{1,0},{0,1},{3,2},{2,3},{5,4},{4,5},{7,6},{6,7},{9,8},{8,9},{11,10... | collective-permute-start | bytes 4718600 | tf_op jit(solution)/shard_map/ppermute | solution.py:205
  2.7 3.7 %collective-permute-start.3 = (bf16[1,64,384]{2,1,0:T(8,128)(2,1)S(1)}, bf16[1,64,384]{2,1,0:T(8,128)(2,1)S(1)}, u32[]{:S(2)}, u32[]{:S(2)}) collective-permute-start(bf16[1,64,384]{2,1,0:T(8,128)(2,1)S(1)} %copy-done.1), channel_id=1, source_target_pairs={{8,0},{9,1},{10,2},{11,3},{12,4},{13,5},{14,6},{15,7},{0,8},{1,9},... | collective-permute-start | bytes 147464 | tf_op jit(solution)/shard_map/ppermute | solution.py:205
  6.4 1.2 %collective-permute-start.2 = (bf16[1,64,384]{2,1,0:T(8,128)(2,1)S(1)}, bf16[1,64,384]{2,1,0:T(8,128)(2,1)S(1)}, u32[]{:S(2)}, u32[]{:S(2)}) collective-permute-start(bf16[1,64,384]{2,1,0:T(8,128)(2,1)S(1)} %copy-done.1), channel_id=1, source_target_pairs={{3,0},{2,1},{1,2},{0,3},{7,4},{6,5},{5,6},{4,7},{11,8},{10,9},{9,1... | collective-permute-start | bytes 147464 | tf_op jit(solution)/shard_map/ppermute | solution.py:205
  7.6 1.6 %collective-permute-start.6 = (bf16[2,64,384]{2,1,0:T(8,128)(2,1)S(1)}, bf16[2,64,384]{2,1,0:T(8,128)(2,1)S(1)}, u32[]{:S(2)}, u32[]{:S(2)}) collective-permute-start(bf16[2,64,384]{2,1,0:T(8,128)(2,1)S(1)} %shard_map.68.refs_0_.own), channel_id=1, source_target_pairs={{6,0},{4,1},{7,2},{5,3},{2,4},{0,5},{3,6},{1,7},{14,8},{12,9},{15,... | collective-permute-start | bytes 294920 | tf_op jit(solution)/shard_map/ppermute | solution.py:205
  9.3 0.0 collective-permute-start.1
  9.3 0.0 collective-permute-done.3.refs_1_
  9.3 1.7 %collective-permute-start.4 = (bf16[1,64,384]{2,1,0:T(8,128)(2,1)S(1)}, bf16[1,64,384]{2,1,0:T(8,128)(2,1)S(1)}, u32[]{:S(2)}, u32[]{:S(2)}) collective-permute-start(bf16[1,64,384]{2,1,0:T(8,128)(2,1)S(1)} %collective-permute-done.3.refs_1_), channel_id=1, source_target_pairs={{2,0},{3,1},{0,2},{1,3},{6,4},{7,5},{4,6},{5,7},{10,8},{11,9},{8,1... | collective-permute-start | bytes 147464 | tf_op jit(solution)/shard_map/ppermute | solution.py:205
  11.0 2.2 %collective-permute-done.6.refs_2_.refs_0_ = bf16[2,64,384]{2,1,0:T(8,128)(2,1)S(1)} collective-permute-done((bf16[2,64,384]{2,1,0:T(8,128)(2,1)S(1)}, bf16[2,64,384]{2,1,0:T(8,128)(2,1)S(1)}, u32[]{:S(2)}, u32[]{:S(2)}) %collective-permute-start.6) | collective-permute-done | bytes 98336 | tf_op jit(solution)/shard_map/ppermute | solution.py:205
  13.3 0.0 collective-permute-done.5.refs_4_
  13.3 2.3 %shard_map.70.refs_5_ = f32[16,1,384]{2,1,0:T(1,128)S(1)} custom-call(bf16[2,64,384]{2,1,0:T(8,128)(2,1)S(1)} %shard_map.68.refs_0_.own, bf16[1,64,384]{2,1,0:T(8,128)(2,1)S(1)} %collective-permute-done.3.refs_1_, bf16[2,64,384]{2,1,0:T(8,128)(2,1)S(1)} %collective-permute-done.6.refs_2_.refs_0_, bf16[32,64,384]{2,1,0:T(8,128)(2,1)S(1)} %copy-done, ...), custom_call_target="tpu_custom_call" | custom-call | flops 805306368 | bytes 3145728 | tf_op jit(solution)/shard_map/pallas_call | solution.py:254
  15.6 0.0 copy-start.2
  15.6 0.0 copy-start.3
  15.6 0.0 collective-permute-done.2.refs_1_.cross
  15.6 0.0 collective-permute-done.4.refs_2_
  15.6 1.5 %collective-permute-done.1.refs_0_.refs_1_ = bf16[2,64,384]{2,1,0:T(8,128)(2,1)S(1)} collective-permute-done((bf16[2,64,384]{2,1,0:T(8,128)(2,1)S(1)}, bf16[2,64,384]{2,1,0:T(8,128)(2,1)S(1)}, u32[]{:S(2)}, u32[]{:S(2)}) %collective-permute-start.1) | collective-permute-done | bytes 98336 | tf_op jit(solution)/shard_map/ppermute | solution.py:205
  17.1 2.3 %shard_map.71 = f32[16,1,384]{2,1,0:T(1,128)S(1)} custom-call(bf16[2,64,384]{2,1,0:T(8,128)(2,1)S(1)} %collective-permute-done.1.refs_0_.refs_1_, bf16[1,64,384]{2,1,0:T(8,128)(2,1)S(1)} %collective-permute-done.2.refs_1_.cross, bf16[1,64,384]{2,1,0:T(8,128)(2,1)S(1)} %collective-permute-done.4.refs_2_, bf16[32,64,384]{2,1,0:T(8,128)(2,1)S(1)} %copy-done, ...), custom_call_target="tpu_custom_call" | custom-call | flops 805306368 | bytes 3145728 | tf_op jit(solution)/shard_map/pallas_call | solution.py:254
  19.4 9.4 %all_to_all.5.got = f32[16,1,384]{2,1,0:T(1,128)S(1)} all-to-all(f32[16,1,384]{2,1,0:T(1,128)S(1)} %shard_map.71), channel_id=1, replica_groups=mesh['rep'=2,'walk'=16] {'walk'}, dimensions={0} | all-to-all | bytes 49152 | tf_op jit(solution)/shard_map/all_to_all | solution.py:266
  28.8 0.0 copy-done.2
  28.8 0.0 copy-done.3
  28.8 0.8 %shard_map.72 = (bf16[2,64,384]{2,1,0:T(8,128)(2,1)}, f32[2]{0:T(128)}, f32[2,512]{1,0:T(2,128)}) custom-call(s32[1,2]{1,0:T(1,128)S(1)} %bitcast.2, s32[1,16]{1,0:T(1,128)S(1)} %bitcast.3, f32[16,1,384]{2,1,0:T(1,128)S(1)} %all_to_all.5.got, bf16[2,64,384]{2,1,0:T(8,128)(2,1)S(1)} %shard_map.68.refs_0_.own, ...), custom_call_target="tpu_custom_call" | custom-call | tf_op jit(solution)/shard_map/pallas_call | solution.py:267
  (3 shorter events, 0.0 us)
Async XLA Ops:
  0.6 1.6 %copy-start.1 = (bf16[1,64,384]{2,1,0:T(8,128)(2,1)S(1)}, bf16[1,64,384]{2,1,0:T(8,128)(2,1)}, u32[]{:S(2)}) copy-start(bf16[1,64,384]{2,1,0:T(8,128)(2,1)} %greens.1) | copy-start | bytes 147460
  0.6 1.6 %copy-start = (bf16[32,64,384]{2,1,0:T(8,128)(2,1)S(1)}, bf16[32,64,384]{2,1,0:T(8,128)(2,1)}, u32[]{:S(2)}) copy-start(bf16[32,64,384]{2,1,0:T(8,128)(2,1)} %refs_3_.3) | copy-start | bytes 4718596
  0.6 1.6 %collective-permute-start = (bf16[1,64,384]{2,1,0:T(8,128)(2,1)}, bf16[1,64,384]{2,1,0:T(8,128)(2,1)S(1)}, u32[]{:S(2)}, u32[]{:S(2)}) collective-permute-start(bf16[1,64,384]{2,1,0:T(8,128)(2,1)} %greens.1), channel_id=1, source_target_pairs={{1,0},{0,1},{3,2},{2,3},{5,4},{4,5},{7,6},{6,7},{9,8},{8,9},{11,10... | collective-permute-start | bytes 147464 | tf_op jit(solution)/shard_map/ppermute | solution.py:205
  2.3 11.0 %collective-permute-start.5 = (bf16[32,64,384]{2,1,0:T(8,128)(2,1)S(1)}, bf16[32,64,384]{2,1,0:T(8,128)(2,1)S(1)}, u32[]{:S(2)}, u32[]{:S(2)}) collective-permute-start(bf16[32,64,384]{2,1,0:T(8,128)(2,1)S(1)} %copy-done), channel_id=1, source_target_pairs={{1,0},{0,1},{3,2},{2,3},{5,4},{4,5},{7,6},{6,7},{9,8},{8,9},{11,10... | collective-permute-start | bytes 4718600 | tf_op jit(solution)/shard_map/ppermute | solution.py:205
  2.7 6.6 %collective-permute-start.3 = (bf16[1,64,384]{2,1,0:T(8,128)(2,1)S(1)}, bf16[1,64,384]{2,1,0:T(8,128)(2,1)S(1)}, u32[]{:S(2)}, u32[]{:S(2)}) collective-permute-start(bf16[1,64,384]{2,1,0:T(8,128)(2,1)S(1)} %copy-done.1), channel_id=1, source_target_pairs={{8,0},{9,1},{10,2},{11,3},{12,4},{13,5},{14,6},{15,7},{0,8},{1,9},... | collective-permute-start | bytes 147464 | tf_op jit(solution)/shard_map/ppermute | solution.py:205
  6.4 9.1 %collective-permute-start.2 = (bf16[1,64,384]{2,1,0:T(8,128)(2,1)S(1)}, bf16[1,64,384]{2,1,0:T(8,128)(2,1)S(1)}, u32[]{:S(2)}, u32[]{:S(2)}) collective-permute-start(bf16[1,64,384]{2,1,0:T(8,128)(2,1)S(1)} %copy-done.1), channel_id=1, source_target_pairs={{3,0},{2,1},{1,2},{0,3},{7,4},{6,5},{5,6},{4,7},{11,8},{10,9},{9,1... | collective-permute-start | bytes 147464 | tf_op jit(solution)/shard_map/ppermute | solution.py:205
  7.6 5.6 %collective-permute-start.6 = (bf16[2,64,384]{2,1,0:T(8,128)(2,1)S(1)}, bf16[2,64,384]{2,1,0:T(8,128)(2,1)S(1)}, u32[]{:S(2)}, u32[]{:S(2)}) collective-permute-start(bf16[2,64,384]{2,1,0:T(8,128)(2,1)S(1)} %shard_map.68.refs_0_.own), channel_id=1, source_target_pairs={{6,0},{4,1},{7,2},{5,3},{2,4},{0,5},{3,6},{1,7},{14,8},{12,9},{15,... | collective-permute-start | bytes 294920 | tf_op jit(solution)/shard_map/ppermute | solution.py:205
  9.3 7.8 %collective-permute-start.1 = (bf16[2,64,384]{2,1,0:T(8,128)(2,1)S(1)}, bf16[2,64,384]{2,1,0:T(8,128)(2,1)S(1)}, u32[]{:S(2)}, u32[]{:S(2)}) collective-permute-start(bf16[2,64,384]{2,1,0:T(8,128)(2,1)S(1)} %shard_map.68.refs_0_.own), channel_id=1, source_target_pairs={{14,0},{12,1},{15,2},{13,3},{10,4},{8,5},{11,6},{9,7},{6,8},{4,9},... | collective-permute-start | bytes 294920 | tf_op jit(solution)/shard_map/ppermute | solution.py:205
  9.3 6.3 %collective-permute-start.4 = (bf16[1,64,384]{2,1,0:T(8,128)(2,1)S(1)}, bf16[1,64,384]{2,1,0:T(8,128)(2,1)S(1)}, u32[]{:S(2)}, u32[]{:S(2)}) collective-permute-start(bf16[1,64,384]{2,1,0:T(8,128)(2,1)S(1)} %collective-permute-done.3.refs_1_), channel_id=1, source_target_pairs={{2,0},{3,1},{0,2},{1,3},{6,4},{7,5},{4,6},{5,7},{10,8},{11,9},{8,1... | collective-permute-start | bytes 147464 | tf_op jit(solution)/shard_map/ppermute | solution.py:205
  15.6 13.2 %copy-start.2 = (s32[2]{0:T(128)S(1)}, s32[2]{0:T(128)}, u32[]{:S(2)}) copy-start(s32[2]{0:T(128)} %param.5) | copy-start | bytes 28
  15.6 13.2 %copy-start.3 = (s32[16]{0:T(128)S(1)}, s32[16]{0:T(128)}, u32[]{:S(2)}) copy-start(s32[16]{0:T(128)} %param.6) | copy-start | bytes 196

commit v6 on v4

--- a/solution.py
+++ b/solution.py
@@ -228,8 +228,7 @@
         compiler_params=params,
         cost_estimate=pl.CostEstimate(flops=0, bytes_accessed=4 * occ * orb, transcendentals=0),
     )(greens, partner)
-    after_own, own = lax.optimization_barrier((cholesky, own))
-    other = permuted(after_own, lambda m, c: (m, 1 - c))
+    other = permuted(cholesky, lambda m, c: (m, 1 - c))
     far = trade(7)
     near = trade(3)
     more = list(range(9, chips, 2))

time: 29.8 us -> 29.3 us (0.983)
  waiting for transfers between devices: 4.85 us -> 2.62 us
  starting transfers between devices: 9.23 us -> 10.6 us
  blocking collectives: 9.46 us -> 9.81 us
    ppermute x7, waiting for transfers between devices: 4.85 us -> 2.62 us  [permuted(): lax.ppermute(x, 'walk', [(2 * n + k, 2 * m + c) for m in range(chips) for...]
    ppermute x7, starting transfers between devices: 9.23 us -> 10.6 us  [permuted(): lax.ppermute(x, 'walk', [(2 * n + k, 2 * m + c) for m in range(chips) for...]
    all_to_all x1, blocking collectives: 9.46 us -> 9.81 us  [body(): got = lax.all_to_all(sent, 'walk', split_axis=0, concat_axis=0, tiled=True)]
where the time goes in v6:
time: 29.3 us; the launch traced here: 29.1 us
  starting transfers between devices  10.6 us (36%)
  blocking collectives  9.81 us (33%)
  Pallas kernels  5.33 us (18%)
  waiting for transfers between devices  2.62 us (9%)
  between operations  0.72 us (2%)
    ppermute x7, starting transfers between devices, permuted(): lax.ppermute(x, 'walk', [(2 * n + k, 2 * m + c) for m in range(chips) for...  10.6 us
    all_to_all x1, blocking collectives, body(): got = lax.all_to_all(sent, 'walk', split_axis=0, concat_axis=0, tiled=True)  9.81 us
    pallas_call x2, Pallas kernels, compute(): pl.pallas_call(functools.partial(compute_kernel, tiles), out_shape=payloa...  4.52 us
    ppermute x7, waiting for transfers between devices, permuted(): lax.ppermute(x, 'walk', [(2 * n + k, 2 * m + c) for m in range(chips) for...  2.62 us
    pallas_call x1, Pallas kernels, body(): pl.pallas_call(functools.partial(final_kernel, -(0.5 / nchol), shifts), o...  0.79 us
  transfers between devices with their start and end apart: 7, of which 3 were waited for; matrix products, arithmetic and copies ran while one was open for 0% of the time, Pallas kernels for 8%

profile of v6, /device:TPU:0, one launch (start us, length us, event | category | flops | bytes accessed | tf_op | source)
XLA Modules:
  0.0 29.1 jit_solution(10940355300377059120)
XLA Ops:
  0.6 0.0 copy-start.1
  0.6 0.5 %collective-permute-start.5 = (bf16[32,64,384]{2,1,0:T(8,128)(2,1)}, bf16[32,64,384]{2,1,0:T(8,128)(2,1)S(1)}, u32[]{:S(2)}, u32[]{:S(2)}) collective-permute-start(bf16[32,64,384]{2,1,0:T(8,128)(2,1)} %refs_3_.3), channel_id=1, source_target_pairs={{1,0},{0,1},{3,2},{2,3},{5,4},{4,5},{7,6},{6,7},{9,8},{8,9},{11,10... | collective-permute-start | bytes 4718600 | tf_op jit(solution)/shard_map/ppermute | solution.py:207
  1.2 0.1 collective-permute-start
  1.2 4.0 %collective-permute-start.3 = (bf16[1,64,384]{2,1,0:T(8,128)(2,1)}, bf16[1,64,384]{2,1,0:T(8,128)(2,1)S(1)}, u32[]{:S(2)}, u32[]{:S(2)}) collective-permute-start(bf16[1,64,384]{2,1,0:T(8,128)(2,1)} %greens.1), channel_id=1, source_target_pairs={{8,0},{9,1},{10,2},{11,3},{12,4},{13,5},{14,6},{15,7},{0,8},{1,9},... | collective-permute-start | bytes 147464 | tf_op jit(solution)/shard_map/ppermute | solution.py:207
  5.3 0.9 %collective-permute-start.2 = (bf16[1,64,384]{2,1,0:T(8,128)(2,1)}, bf16[1,64,384]{2,1,0:T(8,128)(2,1)S(1)}, u32[]{:S(2)}, u32[]{:S(2)}) collective-permute-start(bf16[1,64,384]{2,1,0:T(8,128)(2,1)} %greens.1), channel_id=1, source_target_pairs={{3,0},{2,1},{1,2},{0,3},{7,4},{6,5},{5,6},{4,7},{11,8},{10,9},{9,1... | collective-permute-start | bytes 147464 | tf_op jit(solution)/shard_map/ppermute | solution.py:207
  6.2 0.0 collective-permute-done.partner
  6.2 0.0 copy-done.1
  6.2 0.0 copy-start
  6.2 2.0 %collective-permute-start.6 = (bf16[2,64,384]{2,1,0:T(8,128)(2,1)S(1)}, bf16[2,64,384]{2,1,0:T(8,128)(2,1)S(1)}, u32[]{:S(2)}, u32[]{:S(2)}) collective-permute-start(bf16[2,64,384]{2,1,0:T(8,128)(2,1)S(1)} %shard_map.68.refs_0_.own), channel_id=1, source_target_pairs={{6,0},{4,1},{7,2},{5,3},{2,4},{0,5},{3,6},{1,7},{14,8},{12,9},{15,... | collective-permute-start | bytes 294920 | tf_op jit(solution)/shard_map/ppermute | solution.py:207
  8.2 2.2 %collective-permute-start.1 = (bf16[2,64,384]{2,1,0:T(8,128)(2,1)S(1)}, bf16[2,64,384]{2,1,0:T(8,128)(2,1)S(1)}, u32[]{:S(2)}, u32[]{:S(2)}) collective-permute-start(bf16[2,64,384]{2,1,0:T(8,128)(2,1)S(1)} %shard_map.68.refs_0_.own), channel_id=1, source_target_pairs={{14,0},{12,1},{15,2},{13,3},{10,4},{8,5},{11,6},{9,7},{6,8},{4,9},... | collective-permute-start | bytes 294920 | tf_op jit(solution)/shard_map/ppermute | solution.py:207
  10.4 0.0 collective-permute-done.3.refs_1_
  10.4 0.9 %collective-permute-start.4 = (bf16[1,64,384]{2,1,0:T(8,128)(2,1)S(1)}, bf16[1,64,384]{2,1,0:T(8,128)(2,1)S(1)}, u32[]{:S(2)}, u32[]{:S(2)}) collective-permute-start(bf16[1,64,384]{2,1,0:T(8,128)(2,1)S(1)} %collective-permute-done.3.refs_1_), channel_id=1, source_target_pairs={{2,0},{3,1},{0,2},{1,3},{6,4},{7,5},{4,6},{5,7},{10,8},{11,9},{8,1... | collective-permute-start | bytes 147464 | tf_op jit(solution)/shard_map/ppermute | solution.py:207
  11.3 0.7 %collective-permute-done.6.refs_2_.refs_0_ = bf16[2,64,384]{2,1,0:T(8,128)(2,1)S(1)} collective-permute-done((bf16[2,64,384]{2,1,0:T(8,128)(2,1)S(1)}, bf16[2,64,384]{2,1,0:T(8,128)(2,1)S(1)}, u32[]{:S(2)}, u32[]{:S(2)}) %collective-permute-start.6) | collective-permute-done | bytes 98336 | tf_op jit(solution)/shard_map/ppermute | solution.py:207
  12.0 0.0 collective-permute-done.5.refs_4_
  12.0 0.0 copy-done
  12.0 2.3 %shard_map.70.refs_5_ = f32[16,3,128]{2,1,0:T(4,128)S(1)} custom-call(bf16[2,64,384]{2,1,0:T(8,128)(2,1)S(1)} %shard_map.68.refs_0_.own, bf16[1,64,384]{2,1,0:T(8,128)(2,1)S(1)} %collective-permute-done.3.refs_1_, bf16[2,64,384]{2,1,0:T(8,128)(2,1)S(1)} %collective-permute-done.6.refs_2_.refs_0_, bf16[32,64,384]{2,1,0:T(8,128)(2,1)S(1)} %copy-done, ...), custom_call_target="tpu_custom_call" | custom-call | flops 805306368 | bytes 3145728 | tf_op jit(solution)/shard_map/pallas_call | solution.py:255
  14.3 0.0 copy-start.2
  14.3 0.0 copy-start.3
  14.3 0.0 collective-permute-done.2.refs_1_.cross
  14.3 0.3 %collective-permute-done.4.refs_2_ = bf16[1,64,384]{2,1,0:T(8,128)(2,1)S(1)} collective-permute-done((bf16[1,64,384]{2,1,0:T(8,128)(2,1)S(1)}, bf16[1,64,384]{2,1,0:T(8,128)(2,1)S(1)}, u32[]{:S(2)}, u32[]{:S(2)}) %collective-permute-start.4) | collective-permute-done | bytes 49184 | tf_op jit(solution)/shard_map/ppermute | solution.py:207
  14.6 1.6 %collective-permute-done.1.refs_0_.refs_1_ = bf16[2,64,384]{2,1,0:T(8,128)(2,1)S(1)} collective-permute-done((bf16[2,64,384]{2,1,0:T(8,128)(2,1)S(1)}, bf16[2,64,384]{2,1,0:T(8,128)(2,1)S(1)}, u32[]{:S(2)}, u32[]{:S(2)}) %collective-permute-start.1) | collective-permute-done | bytes 98336 | tf_op jit(solution)/shard_map/ppermute | solution.py:207
  16.2 2.3 %shard_map.71 = f32[16,3,128]{2,1,0:T(4,128)S(1)} custom-call(bf16[2,64,384]{2,1,0:T(8,128)(2,1)S(1)} %collective-permute-done.1.refs_0_.refs_1_, bf16[1,64,384]{2,1,0:T(8,128)(2,1)S(1)} %collective-permute-done.2.refs_1_.cross, bf16[1,64,384]{2,1,0:T(8,128)(2,1)S(1)} %collective-permute-done.4.refs_2_, bf16[32,64,384]{2,1,0:T(8,128)(2,1)S(1)} %copy-done, ...), custom_call_target="tpu_custom_call" | custom-call | flops 805306368 | bytes 3145728 | tf_op jit(solution)/shard_map/pallas_call | solution.py:255
  18.5 9.8 %all_to_all.5.got = f32[16,3,128]{2,1,0:T(4,128)S(1)} all-to-all(f32[16,3,128]{2,1,0:T(4,128)S(1)} %shard_map.71), channel_id=1, replica_groups=mesh['rep'=2,'walk'=16] {'walk'}, dimensions={0} | all-to-all | bytes 49152 | tf_op jit(solution)/shard_map/all_to_all | solution.py:267
  28.3 0.0 copy-done.2
  28.3 0.0 copy-done.3
  28.3 0.8 %shard_map.72 = (bf16[2,64,384]{2,1,0:T(8,128)(2,1)}, f32[2]{0:T(128)}, f32[2,512]{1,0:T(2,128)}) custom-call(s32[1,2]{1,0:T(1,128)S(1)} %bitcast.2, s32[1,16]{1,0:T(1,128)S(1)} %bitcast.3, f32[16,3,128]{2,1,0:T(4,128)S(1)} %all_to_all.5.got, bf16[2,64,384]{2,1,0:T(8,128)(2,1)S(1)} %shard_map.68.refs_0_.own, ...), custom_call_target="tpu_custom_call" | custom-call | tf_op jit(solution)/shard_map/pallas_call | solution.py:268
  (3 shorter events, 0.0 us)
Async XLA Ops:
  0.6 5.6 %copy-start.1 = (bf16[1,64,384]{2,1,0:T(8,128)(2,1)S(1)}, bf16[1,64,384]{2,1,0:T(8,128)(2,1)}, u32[]{:S(2)}) copy-start(bf16[1,64,384]{2,1,0:T(8,128)(2,1)} %greens.1) | copy-start | bytes 147460
  0.6 11.3 %collective-permute-start.5 = (bf16[32,64,384]{2,1,0:T(8,128)(2,1)}, bf16[32,64,384]{2,1,0:T(8,128)(2,1)S(1)}, u32[]{:S(2)}, u32[]{:S(2)}) collective-permute-start(bf16[32,64,384]{2,1,0:T(8,128)(2,1)} %refs_3_.3), channel_id=1, source_target_pairs={{1,0},{0,1},{3,2},{2,3},{5,4},{4,5},{7,6},{6,7},{9,8},{8,9},{11,10... | collective-permute-start | bytes 4718600 | tf_op jit(solution)/shard_map/ppermute | solution.py:207
  1.2 5.0 %collective-permute-start = (bf16[1,64,384]{2,1,0:T(8,128)(2,1)}, bf16[1,64,384]{2,1,0:T(8,128)(2,1)S(1)}, u32[]{:S(2)}, u32[]{:S(2)}) collective-permute-start(bf16[1,64,384]{2,1,0:T(8,128)(2,1)} %greens.1), channel_id=1, source_target_pairs={{1,0},{0,1},{3,2},{2,3},{5,4},{4,5},{7,6},{6,7},{9,8},{8,9},{11,10... | collective-permute-start | bytes 147464 | tf_op jit(solution)/shard_map/ppermute | solution.py:207
  1.2 9.2 %collective-permute-start.3 = (bf16[1,64,384]{2,1,0:T(8,128)(2,1)}, bf16[1,64,384]{2,1,0:T(8,128)(2,1)S(1)}, u32[]{:S(2)}, u32[]{:S(2)}) collective-permute-start(bf16[1,64,384]{2,1,0:T(8,128)(2,1)} %greens.1), channel_id=1, source_target_pairs={{8,0},{9,1},{10,2},{11,3},{12,4},{13,5},{14,6},{15,7},{0,8},{1,9},... | collective-permute-start | bytes 147464 | tf_op jit(solution)/shard_map/ppermute | solution.py:207
  5.3 9.1 %collective-permute-start.2 = (bf16[1,64,384]{2,1,0:T(8,128)(2,1)}, bf16[1,64,384]{2,1,0:T(8,128)(2,1)S(1)}, u32[]{:S(2)}, u32[]{:S(2)}) collective-permute-start(bf16[1,64,384]{2,1,0:T(8,128)(2,1)} %greens.1), channel_id=1, source_target_pairs={{3,0},{2,1},{1,2},{0,3},{7,4},{6,5},{5,6},{4,7},{11,8},{10,9},{9,1... | collective-permute-start | bytes 147464 | tf_op jit(solution)/shard_map/ppermute | solution.py:207
  6.2 5.8 %copy-start = (bf16[32,64,384]{2,1,0:T(8,128)(2,1)S(1)}, bf16[32,64,384]{2,1,0:T(8,128)(2,1)}, u32[]{:S(2)}) copy-start(bf16[32,64,384]{2,1,0:T(8,128)(2,1)} %refs_3_.3) | copy-start | bytes 4718596
  6.2 5.8 %collective-permute-start.6 = (bf16[2,64,384]{2,1,0:T(8,128)(2,1)S(1)}, bf16[2,64,384]{2,1,0:T(8,128)(2,1)S(1)}, u32[]{:S(2)}, u32[]{:S(2)}) collective-permute-start(bf16[2,64,384]{2,1,0:T(8,128)(2,1)S(1)} %shard_map.68.refs_0_.own), channel_id=1, source_target_pairs={{6,0},{4,1},{7,2},{5,3},{2,4},{0,5},{3,6},{1,7},{14,8},{12,9},{15,... | collective-permute-start | bytes 294920 | tf_op jit(solution)/shard_map/ppermute | solution.py:207
  8.2 8.0 %collective-permute-start.1 = (bf16[2,64,384]{2,1,0:T(8,128)(2,1)S(1)}, bf16[2,64,384]{2,1,0:T(8,128)(2,1)S(1)}, u32[]{:S(2)}, u32[]{:S(2)}) collective-permute-start(bf16[2,64,384]{2,1,0:T(8,128)(2,1)S(1)} %shard_map.68.refs_0_.own), channel_id=1, source_target_pairs={{14,0},{12,1},{15,2},{13,3},{10,4},{8,5},{11,6},{9,7},{6,8},{4,9},... | collective-permute-start | bytes 294920 | tf_op jit(solution)/shard_map/ppermute | solution.py:207
  10.4 4.2 %collective-permute-start.4 = (bf16[1,64,384]{2,1,0:T(8,128)(2,1)S(1)}, bf16[1,64,384]{2,1,0:T(8,128)(2,1)S(1)}, u32[]{:S(2)}, u32[]{:S(2)}) collective-permute-start(bf16[1,64,384]{2,1,0:T(8,128)(2,1)S(1)} %collective-permute-done.3.refs_1_), channel_id=1, source_target_pairs={{2,0},{3,1},{0,2},{1,3},{6,4},{7,5},{4,6},{5,7},{10,8},{11,9},{8,1... | collective-permute-start | bytes 147464 | tf_op jit(solution)/shard_map/ppermute | solution.py:207
  14.3 14.0 %copy-start.2 = (s32[2]{0:T(128)S(1)}, s32[2]{0:T(128)}, u32[]{:S(2)}) copy-start(s32[2]{0:T(128)} %param.5) | copy-start | bytes 28
  14.3 14.0 %copy-start.3 = (s32[16]{0:T(128)S(1)}, s32[16]{0:T(128)}, u32[]{:S(2)}) copy-start(s32[16]{0:T(128)} %param.6) | copy-start | bytes 196
